TPU v7x, 32 devices: a whole 2x2x4 slice. The times are simulated.
32 devices in a mesh: snap: 16 (over z, y, x), span: 2 (over core).
Axes of the slice: x: 2, y: 2, z: 4, core: 2. Of those that a mesh axis runs over, the one named last changes fastest.
Arguments:
- features: bfloat16 [2, 32, 512, 512], P('span', 'snap'), may hold values from -6 to 6
- block_values: bfloat16 [2, 32, 4, 4, 128, 128], P('span', 'snap'), may hold values from -0.25 to 0.25
- block_cols: int32 [2, 32, 4, 4], P('span', 'snap'), may hold values from 0 to 3, as said below
- block_counts: int32 [2, 32, 4], P('span', 'snap'), may hold values from 1 to 4, as said below
- band_coeffs: int32 [2, 32, 32], P('span'), may hold values from 1 to 8
- graph_layer_weight: bfloat16 [2, 512, 512], replicated, may hold values from -0.25 to 0.25
- up_weight: bfloat16 [2, 512, 1024], replicated, may hold values from -0.25 to 0.25
- down_weight: bfloat16 [2, 1024, 512], replicated, may hold values from -0.1875 to 0.1875
Outputs:
- vertex_features: bfloat16 [2, 32, 512, 512], P('span', None, 'snap')
Inputs may be any that keep to these rules, and one draw needn't show every extreme that they name: `block_cols`: the block columns named in one block row are distinct, and the first is the row's own block; only the first block_counts entries of a row are used. `block_counts`: block row 0 of every snapshot uses all 4 blocks.
All inputs are finite; a program needn't handle non-finite values.
Results may differ from a plain program's by a relative error of at most 0.018.
Values may be sent and summed in bfloat16 or wider, within the bound.
No kernel may reach another device: no remote copies, remote signals or barrier semaphores. Data moves between devices by JAX's collectives and lax.ppermute only.
A program may use at most 128 MiB of HBM per device.

v0:
```python
import jax
import jax.numpy as jnp
from jax import lax
from jax.sharding import PartitionSpec as P

BAND = 32
LAYERS = 2


def shifted(block, axis, distance):
    devices = range(lax.axis_size(axis))
    route = [(i - distance, i) for i in devices if i - distance in devices]
    return lax.ppermute(block, axis, route)


def local_mixing(band_coeffs):
    span_frames = band_coeffs.shape[1]
    span_index = lax.axis_index("span")
    positions = span_index * span_frames + jnp.arange(span_frames)
    lag_offsets = jnp.arange(BAND)
    valid_lags = (positions[:, None] - lag_offsets[None, :] >= 0).astype(jnp.float32)
    scaled = band_coeffs[0].astype(jnp.float32) * valid_lags
    diagonal_weight_strip = scaled / jnp.sum(scaled, axis=1, keepdims=True)
    lag_index = jnp.arange(span_frames)[:, None] + BAND - jnp.arange(BAND + span_frames)[None, :]
    matches = lag_index[:, :, None] == lag_offsets[None, None, :]
    chosen = jnp.sum(jnp.where(matches, diagonal_weight_strip[:, None, :], 0.0), axis=-1)
    return chosen.astype(jnp.bfloat16)


def sparse_frames(weighted, block_values, block_cols, block_counts):

    def single(frame_rows, frame_values, frame_cols, frame_counts):
        block_total = frame_rows.shape[0] // frame_values.shape[-1]
        blocks = frame_rows.reshape(block_total, frame_values.shape[-1], frame_rows.shape[-1])
        live_slots = jnp.arange(frame_cols.shape[-1])[None, :] < frame_counts[:, None]
        selector = (frame_cols[:, :, None] == jnp.arange(block_total)[None, None, :]) & live_slots[
            :, :, None
        ]
        selector = selector.astype(jnp.bfloat16)
        selected_entries = jnp.einsum(
            "qmn,npd->qmpd", selector, blocks, preferred_element_type=jnp.float32
        ).astype(jnp.bfloat16)
        lag_total_sum = jnp.einsum(
            "qmtp,qmps->qts", frame_values, selected_entries, preferred_element_type=jnp.float32
        )
        return lag_total_sum.reshape(frame_rows.shape).astype(jnp.bfloat16)

    return jax.vmap(single)(weighted, block_values[0], block_cols[0], block_counts[0])


def finish(vertex_rows, earlier, mixing, up_layer, down_layer):
    extended = jnp.concatenate([earlier, vertex_rows], axis=0)
    mixed = jnp.einsum("tj,jkd->tkd", mixing, extended, preferred_element_type=jnp.float32)
    mean_square = jnp.mean(mixed * mixed, axis=-1, keepdims=True)
    normed = (mixed * lax.rsqrt(mean_square + 1e-06)).astype(jnp.bfloat16)
    flat_rows = normed.reshape(-1, normed.shape[-1])
    activated = jax.nn.relu(
        jnp.dot(flat_rows, up_layer, preferred_element_type=jnp.float32)
    ).astype(jnp.bfloat16)
    branch = jnp.dot(activated, down_layer, preferred_element_type=jnp.float32)
    return (mixed + branch.reshape(mixed.shape)).astype(jnp.bfloat16)


def graph_layer(weighted, block_values, block_cols, block_counts, mixing, up_layer, down_layer):
    snaps = lax.axis_size("snap")
    frame_count, vertex_count, width = weighted.shape
    hidden = sparse_frames(weighted, block_values, block_cols, block_counts)
    by_block = hidden.reshape(frame_count, snaps, vertex_count // snaps, width)[None]
    arrived = lax.all_to_all(by_block, "snap", split_axis=2, concat_axis=1, tiled=True)
    vertex_rows = arrived[0, :, 0]
    earlier = shifted(vertex_rows[-BAND:], "span", 1)
    result = finish(vertex_rows, earlier, mixing, up_layer, down_layer)
    return result


def local(
    features,
    block_values,
    block_cols,
    block_counts,
    band_coeffs,
    graph_layer_weight,
    up_weight,
    down_weight,
):
    snaps = lax.axis_size("snap")
    mixing = local_mixing(band_coeffs)
    frames = features[0]
    frame_count, vertex_count, width = frames.shape
    weighted = jnp.dot(frames, graph_layer_weight[0], preferred_element_type=jnp.float32).astype(
        jnp.bfloat16
    )
    layer_out = None
    for layer_index in range(LAYERS):
        layer_out = graph_layer(
            weighted,
            block_values,
            block_cols,
            block_counts,
            mixing,
            up_weight[layer_index],
            down_weight[layer_index],
        )
        if layer_index + 1 < LAYERS:
            sending = jnp.dot(
                layer_out, graph_layer_weight[layer_index + 1], preferred_element_type=jnp.float32
            ).astype(jnp.bfloat16)
            shaped = sending.reshape(snaps, frame_count, sending.shape[1], width)[None]
            returned = lax.all_to_all(shaped, "snap", split_axis=1, concat_axis=3, tiled=True)
            returned = returned.reshape(frame_count, vertex_count, width)
            weighted = returned
    return layer_out[None]


def solution(mesh):
    in_specs = (
        P("span", "snap", None, None),
        P("span", "snap", None, None, None, None),
        P("span", "snap", None, None),
        P("span", "snap", None),
        P("span", None, None),
        P(),
        P(),
        P(),
    )
    out_specs = P("span", None, "snap", None)
    return jax.shard_map(local, mesh=mesh, in_specs=in_specs, out_specs=out_specs, check_vma=False)
```

profile of v0, /device:TPU:1, one launch (start us, length us, event | category | flops | bytes accessed | tf_op | source)
XLA Modules:
  0.0 123.9 jit_solution(774943671296700171)
XLA Ops:
  0.0 0.0 copy-start
  0.0 0.0 copy-start.2
  0.0 0.9 iota_compare_fusion.2
  0.9 2.1 %convolution_convert_fusion.3 = bf16[2,512,512]{2,1,0:T(8,128)(2,1)S(1)} fusion(bf16[1,2,512,512]{3,2,1,0:T(8,128)(2,1)} %param.8, bf16[2,512,512]{2,1,0:T(8,128)(2,1)} %param.13), kind=kOutput, calls=%fused_computation.29 | convolution fusion | flops 537395200 | bytes 2621440 | tf_op jit(solution)/shard_map/dot_general | solution.py:90
  2.9 0.0 copy-done.2
  2.9 1.9 %convolution_convert_fusion.1 = bf16[2,4,4,128,512]{4,2,3,1,0:T(4,128)(2,1)S(1)} fusion(bf16[2,4,128,512,1]{3,2,1,0,4:T(8,128)(2,1)S(1)} %bitcast.99, s32[2,4,4]{2,1,0:T(4,128)S(1)} %bitcast.105, pred[2,4,4]{2,1,0:T(4,128)(4,1)S(1)} %iota_compare_fusion.2), kind=kOutput, calls=%fused_computation.7 | convolution fusion | flops 18874624 | bytes 5243040 | tf_op jit(solution)/shard_map/vmap(qmn,npd->qmpd)/dot_general | solution.py:40
  4.9 0.0 copy-done
  4.9 1.2 bitcast_convert_fusion.1
  6.1 0.1 copy.40
  6.2 0.0 copy-start.1
  6.2 31.7 %all_to_all.45 = bf16[1,2,16,32,512]{4,3,1,0,2:T(8,128)(2,1)S(1)} all-to-all(bf16[1,2,16,32,512]{4,3,1,0,2:T(8,128)(2,1)S(1)} %copy.40), channel_id=1, replica_groups=mesh['snap'=16,'span'=2] {'snap'}, dimensions={2} | all-to-all | bytes 2097152 | tf_op jit(solution)/shard_map/all_to_all | solution.py:69
  37.9 0.6 copy.63
  38.5 1.3 %collective-permute-start = (bf16[32,32,512]{2,0,1:T(8,128)(2,1)S(1)}, bf16[32,32,512]{2,0,1:T(8,128)(2,1)S(1)}, u32[]{:S(2)}, u32[]{:S(2)}) collective-permute-start(bf16[32,32,512]{2,0,1:T(8,128)(2,1)S(1)} %copy.63), channel_id=1, source_target_pairs={{0,1},{2,3},{4,5},{6,7},{8,9},{10,11},{12,13},{14,15},{16,17},{18,... | collective-permute-start | bytes 3145736 | tf_op jit(solution)/shard_map/ppermute | solution.py:13
  39.9 0.0 copy-done.1
  39.9 0.2 fusion.48
  40.0 0.1 iota_subtract_fusion
  40.1 0.1 fusion.47
  40.2 0.2 select_reduce_fusion
  40.4 4.3 %collective-permute-done = bf16[32,32,512]{2,0,1:T(8,128)(2,1)S(1)} collective-permute-done((bf16[32,32,512]{2,0,1:T(8,128)(2,1)S(1)}, bf16[32,32,512]{2,0,1:T(8,128)(2,1)S(1)}, u32[]{:S(2)}, u32[]{:S(2)}) %collective-permute-start) | collective-permute-done | bytes 1048608 | tf_op jit(solution)/shard_map/ppermute | solution.py:13
  44.8 0.5 multiply_reduce_fusion.1
  45.3 0.0 copy-start.3
  45.3 0.2 multiply_convert_fusion.1
  45.5 0.6 copy.42
  46.1 0.8 copy-done.3
  46.9 0.0 copy-start.4
  46.9 1.3 %maximum_convert_fusion.1 = bf16[1024,1024]{1,0:T(8,128)(2,1)S(1)} fusion(bf16[1024,512]{1,0:T(8,128)(2,1)S(1)} %bitcast.101, bf16[2,512,1024]{2,1,0:T(8,128)(2,1)S(1)} %copy-done.3), kind=kOutput, calls=%fused_computation.5 | convolution fusion | flops 1075838976 | bytes 4194304 | tf_op jit(solution)/shard_map/dot_general | solution.py:58
  48.1 0.3 copy-done.4
  48.5 0.0 copy-start.5
  48.5 1.5 %add_convert_fusion.1 = bf16[32,32,512]{2,0,1:T(8,128)(2,1)S(1)} fusion(f32[32,32,512]{2,0,1:T(8,128)S(1)} %get-tuple-element.6, bf16[32,32,1024]{2,1,0:T(8,128)(2,1)S(1)} %bitcast.108, bf16[2,1024,512]{2,1,0:T(8,128)(2,1)S(1)} %copy-done.4), kind=kOutput, calls=%fused_computation.25 | convolution fusion | flops 1074790400 | bytes 6291456 | tf_op jit(solution)/shard_map/dot_general | solution.py:60
  49.9 0.0 copy-done.5
  50.0 0.8 convolution_convert_fusion.2
  50.8 28.1 %all_to_all.46 = bf16[1,16,2,32,512]{4,3,2,0,1:T(8,128)(2,1)S(1)} all-to-all(bf16[1,16,2,32,512]{4,3,2,0,1:T(8,128)(2,1)S(1)} %bitcast.102), channel_id=1, replica_groups=mesh['snap'=16,'span'=2] {'snap'}, dimensions={1} | all-to-all | bytes 2097152 | tf_op jit(solution)/shard_map/all_to_all | solution.py:109
  78.9 0.1 copy.46
  79.0 1.9 %convolution_convert_fusion = bf16[2,4,4,128,512]{4,2,3,1,0:T(4,128)(2,1)S(1)} fusion(bf16[2,4,128,512,1]{3,2,1,0,4:T(8,128)(2,1)S(1)} %bitcast.96, s32[2,4,4]{2,1,0:T(4,128)S(1)} %bitcast.106, pred[2,4,4]{2,1,0:T(4,128)(4,1)S(1)} %iota_compare_fusion.2), kind=kOutput, calls=%fused_computation.6 | convolution fusion | flops 18874624 | bytes 5243040 | tf_op jit(solution)/shard_map/vmap(qmn,npd->qmpd)/dot_general | solution.py:40
  80.9 1.2 %bitcast_convert_fusion = bf16[2,4,512,128]{2,3,1,0:T(8,128)(2,1)S(1)} fusion(bf16[2,4,4,128,512]{4,2,3,1,0:T(4,128)(2,1)S(1)} %convolution_convert_fusion, bf16[1,2,4,4,128,128]{5,4,3,2,1,0:T(8,128)(2,1)S(1)} %copy-done), kind=kOutput, calls=%fused_computation.16 | convolution fusion | flops 537395200 | bytes 6291456 | tf_op jit(solution)/shard_map/vmap(qmtp,qmps->qts)/dot_general | solution.py:43
  82.2 0.1 copy.49
  82.2 29.1 %all_to_all.47 = bf16[1,2,16,32,512]{4,3,1,0,2:T(8,128)(2,1)S(1)} all-to-all(bf16[1,2,16,32,512]{4,3,1,0,2:T(8,128)(2,1)S(1)} %copy.49), channel_id=1, replica_groups=mesh['snap'=16,'span'=2] {'snap'}, dimensions={2} | all-to-all | bytes 2097152 | tf_op jit(solution)/shard_map/all_to_all | solution.py:69
  111.3 0.6 copy.66
  111.9 1.3 %collective-permute-start.1 = (bf16[32,32,512]{2,0,1:T(8,128)(2,1)S(1)}, bf16[32,32,512]{2,0,1:T(8,128)(2,1)S(1)}, u32[]{:S(2)}, u32[]{:S(2)}) collective-permute-start(bf16[32,32,512]{2,0,1:T(8,128)(2,1)S(1)} %copy.66), channel_id=1, source_target_pairs={{0,1},{2,3},{4,5},{6,7},{8,9},{10,11},{12,13},{14,15},{16,17},{18,... | collective-permute-start | bytes 3145736 | tf_op jit(solution)/shard_map/ppermute | solution.py:13
  113.2 5.1 %collective-permute-done.1 = bf16[32,32,512]{2,0,1:T(8,128)(2,1)S(1)} collective-permute-done((bf16[32,32,512]{2,0,1:T(8,128)(2,1)S(1)}, bf16[32,32,512]{2,0,1:T(8,128)(2,1)S(1)}, u32[]{:S(2)}, u32[]{:S(2)}) %collective-permute-start.1) | collective-permute-done | bytes 1048608 | tf_op jit(solution)/shard_map/ppermute | solution.py:13
  118.2 0.5 multiply_reduce_fusion
  118.8 0.2 multiply_convert_fusion
  119.0 0.6 copy.51
  119.6 1.3 %maximum_convert_fusion = bf16[1024,1024]{1,0:T(8,128)(2,1)S(1)} fusion(bf16[1024,512]{1,0:T(8,128)(2,1)S(1)} %bitcast.104, bf16[2,512,1024]{2,1,0:T(8,128)(2,1)S(1)} %copy-done.3), kind=kOutput, calls=%fused_computation.4 | convolution fusion | flops 1075838976 | bytes 4194304 | tf_op jit(solution)/shard_map/dot_general | solution.py:58
  120.8 1.5 %fusion.24 = bf16[1,32,32,512]{3,1,2,0:T(8,128)(2,1)S(1)} fusion(f32[32,32,512]{2,0,1:T(8,128)S(1)} %get-tuple-element.8, bf16[32,32,1024]{2,1,0:T(8,128)(2,1)S(1)} %bitcast.109, bf16[2,1024,512]{2,1,0:T(8,128)(2,1)S(1)} %copy-done.4), kind=kOutput, calls=%fused_computation.30 | convolution fusion | flops 1074790400 | bytes 6291456 | tf_op jit(solution)/shard_map/dot_general | solution.py:60
  122.3 1.6 %copy.53 = bf16[1,32,32,512]{3,2,1,0:T(8,128)(2,1)} copy(bf16[1,32,32,512]{3,1,2,0:T(8,128)(2,1)S(1)} %fusion.24) | data formatting | bytes 2097152 | tf_op jit(solution)/shard_map/broadcast_in_dim | solution.py:112
  (4 shorter events, 0.0 us)
Async XLA Ops:
  0.0 4.9 %copy-start = (bf16[1,2,4,4,128,128]{5,4,3,2,1,0:T(8,128)(2,1)S(1)}, bf16[1,2,4,4,128,128]{5,4,3,2,1,0:T(8,128)(2,1)}, u32[]{:S(2)}) copy-start(bf16[1,2,4,4,128,128]{5,4,3,2,1,0:T(8,128)(2,1)} %param.9) | copy-start | bytes 3145732
  0.0 2.9 %copy-start.2 = (s32[1,2,4,4]{3,2,1,0:T(4,128)S(1)}, s32[1,2,4,4]{3,2,1,0:T(4,128)}, u32[]{:S(2)}) copy-start(s32[1,2,4,4]{3,2,1,0:T(4,128)} %param.10) | copy-start | bytes 388
  6.2 33.7 %copy-start.1 = (s32[1,32,32]{2,1,0:T(8,128)S(1)}, s32[1,32,32]{2,1,0:T(8,128)}, u32[]{:S(2)}) copy-start(s32[1,32,32]{2,1,0:T(8,128)} %param.12) | copy-start | bytes 12292
  38.5 6.2 %collective-permute-start = (bf16[32,32,512]{2,0,1:T(8,128)(2,1)S(1)}, bf16[32,32,512]{2,0,1:T(8,128)(2,1)S(1)}, u32[]{:S(2)}, u32[]{:S(2)}) collective-permute-start(bf16[32,32,512]{2,0,1:T(8,128)(2,1)S(1)} %copy.63), channel_id=1, source_target_pairs={{0,1},{2,3},{4,5},{6,7},{8,9},{10,11},{12,13},{14,15},{16,17},{18,... | collective-permute-start | bytes 3145736 | tf_op jit(solution)/shard_map/ppermute | solution.py:13
  45.3 1.6 %copy-start.3 = (bf16[2,512,1024]{2,1,0:T(8,128)(2,1)S(1)}, bf16[2,512,1024]{2,1,0:T(8,128)(2,1)}, u32[]{:S(2)}) copy-start(bf16[2,512,1024]{2,1,0:T(8,128)(2,1)} %param.14) | copy-start | bytes 6291460
  46.9 1.6 %copy-start.4 = (bf16[2,1024,512]{2,1,0:T(8,128)(2,1)S(1)}, bf16[2,1024,512]{2,1,0:T(8,128)(2,1)}, u32[]{:S(2)}) copy-start(bf16[2,1024,512]{2,1,0:T(8,128)(2,1)} %param.15) | copy-start | bytes 6291460
  48.5 1.5 %copy-start.5 = (bf16[2,512,512]{2,1,0:T(8,128)(2,1)S(1)}, bf16[2,512,512]{2,1,0:T(8,128)(2,1)}, u32[]{:S(2)}) copy-start(bf16[2,512,512]{2,1,0:T(8,128)(2,1)} %param.13) | copy-start | bytes 3145732
  111.9 6.4 %collective-permute-start.1 = (bf16[32,32,512]{2,0,1:T(8,128)(2,1)S(1)}, bf16[32,32,512]{2,0,1:T(8,128)(2,1)S(1)}, u32[]{:S(2)}, u32[]{:S(2)}) collective-permute-start(bf16[32,32,512]{2,0,1:T(8,128)(2,1)S(1)} %copy.66), channel_id=1, source_target_pairs={{0,1},{2,3},{4,5},{6,7},{8,9},{10,11},{12,13},{14,15},{16,17},{18,... | collective-permute-start | bytes 3145736 | tf_op jit(solution)/shard_map/ppermute | solution.py:13
where the time goes:
time: 124 us
  blocking collectives  88.9 us (72%)
  matrix products  15.7 us (13%)
  waiting for transfers between devices  9.38 us (8%)
  local copies, waits for them, and re-layouts  5.21 us (4%)
  starting transfers between devices  2.58 us (2%)
  other arithmetic  1.87 us (2%)
    all_to_all x2, blocking collectives, graph_layer(): lax.all_to_all(by_block, 'snap', split_axis=2, concat_axis=1, tiled=True)  60.8 us
    all_to_all x1, blocking collectives, local(): lax.all_to_all(shaped, 'snap', split_axis=1, concat_axis=3, tiled=True)  28.1 us
    ppermute x2, waiting for transfers between devices, shifted(): return lax.ppermute(block, axis, route)  9.38 us
    dot_general x2, matrix products, single(): jnp.einsum('qmn,npd->qmpd', selector, blocks, preferred_element_type=jnp....  3.84 us
    dot_general x2, matrix products, finish(): branch = jnp.dot(activated, down_layer, preferred_element_type=jnp.float32)  2.96 us
    ppermute x2, starting transfers between devices, shifted(): return lax.ppermute(block, axis, route)  2.58 us
    dot_general x2, matrix products, finish(): jnp.dot(flat_rows, up_layer, preferred_element_type=jnp.float32)  2.5 us
  transfers between devices with their start and end apart: 2, of which 2 were waited for; matrix products, arithmetic and copies ran while one was open for 0% of the time, Pallas kernels for 0%

commit v1 on v0

v1 whole, which is shorter than its diff:
```python
import functools

import jax
import jax.numpy as jnp
from jax import lax
from jax.experimental import pallas as pl
from jax.experimental.pallas import tpu as pltpu
from jax.sharding import PartitionSpec as P

BAND = 32
LAYERS = 2
TILE = 256
REACH = 3
ROWS = 512
EVERY = ("snap", "span")
MIB = 1 << 20


def dot(left, right):
    return jnp.dot(left, right, preferred_element_type=jnp.float32)


def in_vmem(shape, dtype=jnp.bfloat16):
    return pltpu.VMEM(shape, dtype)


def vmem_specs(count):
    return [pl.BlockSpec(memory_space=pltpu.VMEM)] * count


def held(array):
    return pltpu.with_memory_space_constraint(array, pltpu.VMEM)


def in_hbm(array):
    return pltpu.with_memory_space_constraint(array, pltpu.HBM)


def hbm_specs(count):
    return [pl.BlockSpec(memory_space=pltpu.HBM)] * count


def params(mib=16):
    return pltpu.CompilerParams(vmem_limit_bytes=mib * MIB)


def propagate(frame, values_ref, cols_ref, counts_ref, weighted_ref, dense_ref, sent_ref):
    block_rows, slots, size, _ = values_ref.shape[1:]
    group = dense_ref.shape[0] // size
    own = sent_ref.shape[2]
    width = sent_ref.shape[3]
    for first in range(0, block_rows, group):
        dense_ref[...] = jnp.zeros_like(dense_ref)
        for row in range(group):
            for slot in range(slots):

                @pl.when(slot < counts_ref[frame, first + row])
                def place():
                    column = pl.multiple_of(cols_ref[frame, first + row, slot] * size, size)
                    dense_ref[pl.ds(row * size, size), pl.ds(column, size)] = values_ref[
                        frame, first + row, slot
                    ]

        summed = dot(dense_ref[...], weighted_ref[...]).astype(jnp.bfloat16)
        owners = group * size // own
        sent_ref[pl.ds(first * size // own, owners), frame] = summed.reshape(owners, own, width)


def copies(pairs, sems):
    return [pltpu.make_async_copy(*pair, sems.at[place]) for place, pair in enumerate(pairs)]


def first_kernel(
    features_ref,
    weight_ref,
    values_ref,
    cols_ref,
    counts_ref,
    sent_ref,
    features_in,
    weight_in,
    values_in,
    cols_in,
    counts_in,
    weighted_ref,
    dense_ref,
    sems,
):
    frames = range(features_in.shape[0])
    loads = copies(
        [(weight_ref.at[0], weight_in)]
        + [(features_ref.at[0, frame], features_in.at[frame]) for frame in frames]
        + [(cols_ref.at[0], cols_in), (counts_ref.at[0], counts_in)]
        + [(values_ref.at[0, frame], values_in.at[frame]) for frame in frames],
        sems,
    )
    for load in loads:
        load.start()
    loads[0].wait()
    for frame in frames:
        loads[1 + frame].wait()
        weighted_ref[...] = dot(features_in[frame], weight_in[...]).astype(jnp.bfloat16)
        if frame == 0:
            loads[1 + len(frames)].wait()
            loads[2 + len(frames)].wait()
        loads[3 + len(frames) + frame].wait()
        propagate(frame, values_in, cols_in, counts_in, weighted_ref, dense_ref, sent_ref)


def later_kernel(
    arrived_ref, values_ref, cols_ref, counts_ref, sent_ref, weighted_ref, dense_ref
):
    for frame in range(arrived_ref.shape[1]):
        weighted_ref[...] = arrived_ref[:, frame].reshape(weighted_ref.shape)
        propagate(frame, values_ref, cols_ref, counts_ref, weighted_ref, dense_ref, sent_ref)


def graph_scratch(values, width):
    block_rows, _, size, _ = values.shape[-4:]
    vertices = block_rows * size
    return [
        pltpu.VMEM((vertices, width), jnp.bfloat16),
        pltpu.VMEM((min(block_rows, 4) * size, vertices), jnp.bfloat16),
    ]


def first_graph(features, weight, values, cols, counts, owners):
    frames, vertices, width = features.shape[1:]
    return pl.pallas_call(
        first_kernel,
        name="first_graph",
        out_shape=in_vmem((owners, frames, vertices // owners, width)),
        in_specs=hbm_specs(5),
        out_specs=pl.BlockSpec(memory_space=pltpu.VMEM),
        scratch_shapes=[
            pltpu.VMEM(features.shape[1:], jnp.bfloat16),
            pltpu.VMEM(weight.shape[1:], jnp.bfloat16),
            pltpu.VMEM(values.shape[1:], jnp.bfloat16),
            pltpu.SMEM(cols.shape[1:], jnp.int32),
            pltpu.SMEM(counts.shape[1:], jnp.int32),
            *graph_scratch(values, width),
            pltpu.SemaphoreType.DMA((3 + 2 * frames,)),
        ],
        compiler_params=params(32),
    )(*map(in_hbm, (features, weight, values, cols, counts)))


def later_graph(arrived, values, cols, counts):
    smem = pl.BlockSpec(memory_space=pltpu.SMEM)
    return pl.pallas_call(
        later_kernel,
        name="later_graph",
        out_shape=in_vmem(arrived.shape),
        in_specs=vmem_specs(2) + [smem, smem],
        out_specs=pl.BlockSpec(memory_space=pltpu.VMEM),
        scratch_shapes=graph_scratch(values, arrived.shape[-1]),
        compiler_params=params(),
    )(held(arrived), held(values), cols, counts)


def band_weights(coeffs, frames_in_tile):
    frames = coeffs.shape[0]
    back = (REACH - 1) * frames_in_tile
    lags = jnp.arange(BAND)
    valid = jnp.arange(frames)[:, None] - lags[None, :] >= 0
    scaled = jnp.where(valid, coeffs.astype(jnp.float32), 0.0)
    weights = scaled / jnp.sum(scaled, axis=1, keepdims=True)
    lag = back + (jnp.arange(frames) % frames_in_tile)[:, None] - jnp.arange(
        REACH * frames_in_tile
    )
    chosen = jnp.where(lag[:, :, None] == lags, weights[:, None, :], 0.0)
    return jnp.sum(chosen, axis=-1).astype(jnp.bfloat16)


def spread_kernel(own, weights_ref, tiles_ref):
    tiles, reach, rows, _ = tiles_ref.shape
    in_tile = rows // own
    spread = (
        lax.broadcasted_iota(jnp.int32, (rows, in_tile), 0) // own
        == lax.broadcasted_iota(jnp.int32, (rows, in_tile), 1)
    ).astype(jnp.bfloat16)
    same = (
        lax.broadcasted_iota(jnp.int32, (rows, rows), 0) % own
        == lax.broadcasted_iota(jnp.int32, (rows, rows), 1) % own
    )
    for tile in range(tiles):
        down = dot(spread, weights_ref[pl.ds(tile * in_tile, in_tile)]).astype(jnp.bfloat16)
        for source in range(reach):
            part = down[:, source * in_tile : (source + 1) * in_tile]
            across = lax.dot_general(
                part, spread, (((1,), (1,)), ((), ())), preferred_element_type=jnp.float32
            )
            tiles_ref[tile, source] = jnp.where(same, across, 0.0).astype(jnp.bfloat16)


def spread_band(weights, own):
    tiles = weights.shape[0] * own // TILE
    return pl.pallas_call(
        functools.partial(spread_kernel, own),
        name="spread_band",
        out_shape=jax.ShapeDtypeStruct((tiles, REACH, TILE, TILE), jnp.bfloat16),
        in_specs=vmem_specs(1),
        out_specs=pl.BlockSpec(memory_space=pltpu.VMEM),
        compiler_params=params(),
    )(weights)


def rows_of(ref, tile, steps):
    in_span = ref.shape[0] // steps
    first = (tile % in_span) * steps
    return (pl.ds(first, steps), tile // in_span)


def mix(place, band_tile, sources, mixed_ref, normed_ref):
    total = None
    for part, source in sources:
        term = dot(band_tile[part], source)
        total = term if total is None else total + term
    mean_square = jnp.mean(total * total, axis=-1, keepdims=True)
    rows = pl.ds(place * TILE, TILE)
    mixed_ref[rows] = total
    normed_ref[rows] = (total * lax.rsqrt(mean_square + 1e-06)).astype(jnp.bfloat16)


def perceptron(mixed_ref, normed_ref, up, down):
    active = jnp.maximum(dot(normed_ref[...], up), 0.0).astype(jnp.bfloat16)
    return (mixed_ref[...] + dot(active, down)).astype(jnp.bfloat16)


def middle_kernel(
    layer,
    arrived_ref,
    band_ref,
    up_ref,
    down_ref,
    next_ref,
    sent_ref,
    band_in,
    up_in,
    down_in,
    next_in,
    mixed_ref,
    normed_ref,
    sems,
):
    tiles, steps = band_ref.shape[0], TILE // (arrived_ref.shape[2] * arrived_ref.shape[3])
    width = mixed_ref.shape[1]
    together = ROWS // TILE
    loads = copies(
        [(band_ref.at[tile], band_in.at[tile]) for tile in range(tiles)]
        + [
            (up_ref.at[layer], up_in),
            (down_ref.at[layer], down_in),
            (next_ref.at[layer + 1], next_in),
        ],
        sems,
    )
    order = [*range(together), tiles, tiles + 1, tiles + 2, *range(together, tiles)]
    for place in order:
        loads[place].start()
    for first in range(0, tiles, together):
        for place, tile in enumerate(range(first, first + together)):
            loads[tile].wait()
            sources = [
                (
                    REACH - 1 - back,
                    arrived_ref[rows_of(arrived_ref, tile - back, steps)].reshape(TILE, width),
                )
                for back in range(min(REACH, tile + 1))
            ]
            mix(place, band_in.at[tile], sources, mixed_ref, normed_ref)
        if first == 0:
            loads[tiles].wait()
            loads[tiles + 1].wait()
        layer_out = perceptron(mixed_ref, normed_ref, up_in[...], down_in[...])
        if first == 0:
            loads[tiles + 2].wait()
        result = dot(layer_out, next_in[...]).astype(jnp.bfloat16)
        result = result.reshape(together, steps, *sent_ref.shape[2:])
        for place in range(together):
            sent_ref[rows_of(sent_ref, first + place, steps)] = result[place]


def row_scratch(width):
    return [pltpu.VMEM((ROWS, width), jnp.float32), pltpu.VMEM((ROWS, width), jnp.bfloat16)]


def middle_stage(layer, arrived, band, up, down, following):
    width = up.shape[1]
    return pl.pallas_call(
        functools.partial(middle_kernel, layer),
        name="middle_stage",
        out_shape=in_vmem(arrived.shape),
        in_specs=vmem_specs(1) + hbm_specs(4),
        out_specs=pl.BlockSpec(memory_space=pltpu.VMEM),
        scratch_shapes=[
            pltpu.VMEM(band.shape, jnp.bfloat16),
            *(pltpu.VMEM(array.shape[1:], jnp.bfloat16) for array in (up, down, following)),
            *row_scratch(width),
            pltpu.SemaphoreType.DMA((band.shape[0] + 3,)),
        ],
        compiler_params=params(24),
    )(held(arrived), *map(in_hbm, (band, up, down, following)))


def last_kernel(
    layer, flip, arrived_ref, band_ref, up_ref, down_ref, out_ref, mixed_ref, normed_ref
):
    span = lax.axis_index("span")
    span = 1 - span if flip else span
    steps = TILE // (arrived_ref.shape[2] * arrived_ref.shape[3])
    in_span = arrived_ref.shape[0] // steps
    width = mixed_ref.shape[1]
    own = arrived_ref.shape[3]
    frames = TILE // own
    together = ROWS // TILE
    for first in range(0, in_span, together):
        for place in range(together):
            tile = span * in_span + first + place
            sources = [
                (
                    REACH - 1 - back,
                    arrived_ref[
                        rows_of(arrived_ref, jnp.maximum(tile - back, 0), steps)
                    ].reshape(TILE, width),
                )
                for back in range(REACH)
            ]
            mix(place, band_ref.at[tile], sources, mixed_ref, normed_ref)
        layer_out = perceptron(mixed_ref, normed_ref, up_ref[layer], down_ref[layer])
        out_ref[pl.ds(first * frames, together * frames)] = layer_out.reshape(
            together * frames, own, width
        )


def last_stage(layer, flip, arrived, band, up, down):
    width = up.shape[1]
    owners, _, frames, own, _ = arrived.shape
    return pl.pallas_call(
        functools.partial(last_kernel, layer, flip),
        name="last_stage",
        out_shape=in_vmem((owners * frames, own, width)),
        in_specs=vmem_specs(4),
        out_specs=pl.BlockSpec(memory_space=pltpu.VMEM),
        scratch_shapes=row_scratch(width),
        compiler_params=params(),
    )(held(arrived), held(band), held(up), held(down))


def assemble_kernel(kept_ref, received_ref, out_ref, sems):
    span = lax.axis_index("span")
    loads = copies(
        [(kept_ref, out_ref.at[:, span]), (received_ref, out_ref.at[:, 1 - span])], sems
    )
    for load in loads:
        load.start()
    for load in loads:
        load.wait()


def assemble(kept, received):
    frames, own, width = kept.shape
    return pl.pallas_call(
        assemble_kernel,
        name="assemble",
        out_shape=pltpu.HBM((frames, 2, own, width), jnp.bfloat16),
        in_specs=vmem_specs(2),
        out_specs=hbm_specs(1)[0],
        scratch_shapes=[pltpu.SemaphoreType.DMA((2,))],
        compiler_params=params(),
    )(held(kept), held(received))


def exchange(blocks):
    return lax.all_to_all(blocks, EVERY, split_axis=0, concat_axis=0, tiled=True)


def local(
    features,
    block_values,
    block_cols,
    block_counts,
    band_coeffs,
    graph_layer_weight,
    up_weight,
    down_weight,
):
    snaps, spans = lax.axis_size("snap"), lax.axis_size("span")
    span = lax.axis_index("span")
    swap = [(0, 1), (1, 0)]
    owners = snaps * spans
    frames, vertices, width = features.shape[1:]
    own = vertices // owners
    by_owner = (snaps, spans, frames, own, width)

    sent = first_graph(
        features, graph_layer_weight, block_values, block_cols, block_counts, owners
    )
    other_coeffs = lax.ppermute(band_coeffs[0], "span", swap)
    ordered = jnp.where(
        span == 0,
        jnp.concatenate([band_coeffs[0], other_coeffs]),
        jnp.concatenate([other_coeffs, band_coeffs[0]]),
    )
    band = spread_band(band_weights(ordered, TILE // own), own)
    for layer in range(LAYERS - 1):
        arrived = exchange(sent).reshape(by_owner)
        sent = middle_stage(layer, arrived, band, up_weight, down_weight, graph_layer_weight)
        arrived = exchange(sent.reshape(owners, frames, own, width))
        sent = later_graph(arrived, block_values[0], block_cols[0], block_counts[0])
    arrived = exchange(sent).reshape(by_owner)
    give = last_stage(LAYERS - 1, True, arrived, band, up_weight, down_weight)
    received = lax.ppermute(give, "span", swap)
    kept = last_stage(LAYERS - 1, False, arrived, band, up_weight, down_weight)
    return assemble(kept, received).reshape(1, snaps * frames, spans * own, width)


def solution(mesh):
    in_specs = (
        P("span", "snap", None, None),
        P("span", "snap", None, None, None, None),
        P("span", "snap", None, None),
        P("span", "snap", None),
        P("span", None, None),
        P(),
        P(),
        P(),
    )
    out_specs = P("span", None, "snap", None)
    return jax.shard_map(local, mesh=mesh, in_specs=in_specs, out_specs=out_specs, check_vma=False)
```

time: 124 us -> 110 us (0.89)
  blocking collectives: 88.9 us -> 59.3 us
  Pallas kernels: 0 us -> 17.9 us
  matrix products: 15.7 us -> 0 us
  waiting for transfers between devices: 9.38 us -> 22.1 us
  starting transfers between devices: 2.58 us -> 8.57 us
  local copies, waits for them, and re-layouts: 5.21 us -> 1.36 us
  other arithmetic: 1.87 us -> 0.39 us
    all_to_all x3 -> x2, blocking collectives: 88.9 us -> 59.3 us  [exchange(): lax.all_to_all(blocks, EVERY, split_axis=0, concat_axis=0, tiled=True)]
    all_to_all x0 -> x1, waiting for transfers between devices: none -> 21.2 us  [exchange(): lax.all_to_all(blocks, EVERY, split_axis=0, concat_axis=0, tiled=True)]
    pallas_call x0 -> x7, Pallas kernels: none -> 17.9 us  [the longest x1 5.83 us: middle_stage(): pl.pallas_call(functools.partial(middle_kernel, layer), name='middle_stag...]
    dot_general x12 -> x0, matrix products: 15.7 us -> none  [the longest x2 3.84 us: single(): jnp.einsum('qmn,npd->qmpd', selector, blocks, preferred_element_type=jnp....]
    ppermute x2, waiting for transfers between devices: 9.38 us -> 0.91 us  [the longest x1 0.91 us: local(): other_coeffs = lax.ppermute(band_coeffs[0], 'span', swap)]
    all_to_all x0 -> x1, starting transfers between devices: none -> 7.07 us  [exchange(): lax.all_to_all(blocks, EVERY, split_axis=0, concat_axis=0, tiled=True)]
    broadcast_in_dim x1 -> x0, local copies, waits for them, and re-layouts: 1.55 us -> none  [local(): return layer_out[None]]
  transfers between devices with their start and end apart: 2 -> 3, of which waited for: 2 -> 2; matrix products, arithmetic and copies ran while one was open for 0% -> 1% of each run, Pallas kernels for 0% -> 3%
where the time goes in v1:
time: 110 us
  blocking collectives  59.3 us (54%)
  waiting for transfers between devices  22.1 us (20%)
  Pallas kernels  17.9 us (16%)
  starting transfers between devices  8.57 us (8%)
  local copies, waits for them, and re-layouts  1.36 us (1%)
    all_to_all x2, blocking collectives, exchange(): lax.all_to_all(blocks, EVERY, split_axis=0, concat_axis=0, tiled=True)  59.3 us
    all_to_all x1, waiting for transfers between devices, exchange(): lax.all_to_all(blocks, EVERY, split_axis=0, concat_axis=0, tiled=True)  21.2 us
    all_to_all x1, starting transfers between devices, exchange(): lax.all_to_all(blocks, EVERY, split_axis=0, concat_axis=0, tiled=True)  7.07 us
    pallas_call x1, Pallas kernels, middle_stage(): pl.pallas_call(functools.partial(middle_kernel, layer), name='middle_stag...  5.83 us
    pallas_call x1, Pallas kernels, first_graph(): pl.pallas_call(first_kernel, name='first_graph', out_shape=in_vmem((owner...  4.44 us
    pallas_call x2, Pallas kernels, last_stage(): pl.pallas_call(functools.partial(last_kernel, layer, flip), name='last_st...  3.54 us
  transfers between devices with their start and end apart: 3, of which 2 were waited for; matrix products, arithmetic and copies ran while one was open for 1% of the time, Pallas kernels for 3%

profile of v1, /device:TPU:1, one launch (start us, length us, event | category | flops | bytes accessed | tf_op | source)
XLA Modules:
  0.0 109.8 jit_solution(8549377995290838894)
XLA Ops:
  0.0 4.4 %first_graph.1 = bf16[32,2,16,512]{3,2,1,0:T(8,128)(2,1)} custom-call(bf16[1,2,512,512]{3,2,1,0:T(8,128)(2,1)} %features_ref.1, bf16[2,512,512]{2,1,0:T(8,128)(2,1)} %next_ref.1, bf16[1,2,4,4,128,128]{5,4,3,2,1,0:T(8,128)(2,1)} %values_ref.1, s32[1,2,4,4]{3,2,1,0:T(4,128)} %cols_ref.1, s32[1,2,4]{2,1,0:T(2,128)} %counts_ref.1), custom_call_target="tpu_custom_call" | custom-call | tf_op jit(solution)/shard_map/first_graph/pallas_call | solution.py:129
  4.5 0.0 copy-start.7
  4.5 7.1 %all-to-all-start = ((bf16[32,2,16,512]{3,2,1,0:T(8,128)(2,1)}), bf16[32,2,16,512]{3,2,1,0:T(8,128)(2,1)S(1)}, u32[]{:S(2)}, u32[]{:S(2)}) async-start(bf16[32,2,16,512]{3,2,1,0:T(8,128)(2,1)} %first_graph.1), calls=%async_computation | async-start | bytes 2097152 | tf_op jit(solution)/shard_map/all_to_all | solution.py:375
  11.5 0.0 copy-done.7
  11.5 0.1 copy.11
  11.6 0.3 collective-permute-start
  11.9 0.9 collective-permute-done
  12.8 0.1 fusion.3
  12.9 0.1 broadcast_divide_fusion
  13.0 0.2 select_reduce_fusion
  13.2 0.1 copy.12.weights_ref
  13.3 1.2 %spread_band.1.band_ref = bf16[4,3,256,256]{3,2,1,0:T(8,128)(2,1)S(1)} custom-call(bf16[64,48]{1,0:T(8,128)(2,1)S(1)} %copy.12.weights_ref), custom_call_target="tpu_custom_call" | custom-call | tf_op jit(solution)/shard_map/spread_band/pallas_call | solution.py:198
  14.5 0.0 copy-start
  14.5 1.1 %copy-done = bf16[4,3,256,256]{3,2,1,0:T(8,128)(2,1)} copy-done((bf16[4,3,256,256]{3,2,1,0:T(8,128)(2,1)}, bf16[4,3,256,256]{3,2,1,0:T(8,128)(2,1)S(1)}, u32[]{:S(2)}) %copy-start) | copy-done | bytes 1572888
  15.6 21.2 %all-to-all-done = bf16[32,2,16,512]{3,2,1,0:T(8,128)(2,1)S(1)} async-done(((bf16[32,2,16,512]{3,2,1,0:T(8,128)(2,1)}), bf16[32,2,16,512]{3,2,1,0:T(8,128)(2,1)S(1)}, u32[]{:S(2)}, u32[]{:S(2)}) %all-to-all-start) | async-done | bytes 1048608 | tf_op jit(solution)/shard_map/all_to_all | solution.py:375
  36.9 5.8 %middle_stage.1 = bf16[16,2,2,16,512]{4,3,2,1,0:T(8,128)(2,1)S(1)} custom-call(bf16[16,2,2,16,512]{4,3,2,1,0:T(8,128)(2,1)S(1)} %bitcast.10, bf16[4,3,256,256]{3,2,1,0:T(8,128)(2,1)} %copy-done, bf16[2,512,1024]{2,1,0:T(8,128)(2,1)} %up_ref.5, bf16[2,1024,512]{2,1,0:T(8,128)(2,1)} %down_ref.5, bf16[2,512,512]{2,1,0:T(8,128)(2,1)} %next_ref.1), custom_call_target="tpu_custom_call" | custom-call | tf_op jit(solution)/shard_map/middle_stage/pallas_call | solution.py:290
  42.7 0.0 copy-start.4
  42.7 0.0 copy-start.5
  42.7 0.0 copy-start.6
  42.7 0.0 copy-start.3
  42.8 29.7 %all_to_all.15.arrived_ref = bf16[32,2,16,512]{3,2,1,0:T(8,128)(2,1)S(1)} all-to-all(bf16[32,2,16,512]{3,2,1,0:T(8,128)(2,1)S(1)} %bitcast.11), channel_id=1, replica_groups=mesh['snap'=16,'span'=2] {'snap','span'}, dimensions={0} | all-to-all | bytes 2097152 | tf_op jit(solution)/shard_map/all_to_all | solution.py:375
  72.4 0.0 copy-done.4
  72.4 0.0 copy-done.5
  72.4 0.0 copy-done.6
  72.4 0.0 copy-start.1
  72.4 0.0 copy-start.2
  72.5 1.9 %later_graph.1 = bf16[32,2,16,512]{3,2,1,0:T(8,128)(2,1)S(1)} custom-call(bf16[32,2,16,512]{3,2,1,0:T(8,128)(2,1)S(1)} %all_to_all.15.arrived_ref, bf16[2,4,4,128,128]{4,3,2,1,0:T(8,128)(2,1)S(1)} %bitcast.12, s32[2,4,4]{2,1,0:T(4,128)S(1)} %bitcast.13, s32[2,4]{1,0:T(2,128)S(1)} %bitcast.14), custom_call_target="tpu_custom_call" | custom-call | tf_op jit(solution)/shard_map/later_graph/pallas_call | solution.py:150
  74.4 29.6 %all_to_all.16 = bf16[32,2,16,512]{3,2,1,0:T(8,128)(2,1)S(1)} all-to-all(bf16[32,2,16,512]{3,2,1,0:T(8,128)(2,1)S(1)} %later_graph.1), channel_id=1, replica_groups=mesh['snap'=16,'span'=2] {'snap','span'}, dimensions={0} | all-to-all | bytes 2097152 | tf_op jit(solution)/shard_map/all_to_all | solution.py:375
  104.0 0.0 copy-done.3
  104.0 0.0 copy-done.1
  104.0 0.0 copy-done.2
  104.0 1.8 %last_stage.3 = bf16[32,16,512]{2,1,0:T(8,128)(2,1)S(1)} custom-call(bf16[16,2,2,16,512]{4,3,2,1,0:T(8,128)(2,1)S(1)} %bitcast.8, bf16[4,3,256,256]{3,2,1,0:T(8,128)(2,1)S(1)} %copy-done.1, bf16[2,512,1024]{2,1,0:T(8,128)(2,1)S(1)} %copy-done.2, bf16[2,1024,512]{2,1,0:T(8,128)(2,1)S(1)} %copy-done.3), custom_call_target="tpu_custom_call" | custom-call | tf_op jit(solution)/shard_map/last_stage/pallas_call | solution.py:339
  105.8 1.2 %collective-permute-start.1 = (bf16[32,16,512]{2,1,0:T(8,128)(2,1)S(1)}, bf16[32,16,512]{2,1,0:T(8,128)(2,1)S(1)}, u32[]{:S(2)}, u32[]{:S(2)}) collective-permute-start(bf16[32,16,512]{2,1,0:T(8,128)(2,1)S(1)} %last_stage.3), channel_id=1, source_target_pairs={{0,1},{1,0},{2,3},{3,2},{4,5},{5,4},{6,7},{7,6},{8,9},{9,8},{10,11... | collective-permute-start | bytes 1572872 | tf_op jit(solution)/shard_map/ppermute | solution.py:413
  107.1 1.8 %last_stage.2.kept_ref = bf16[32,16,512]{2,1,0:T(8,128)(2,1)S(1)} custom-call(bf16[16,2,2,16,512]{4,3,2,1,0:T(8,128)(2,1)S(1)} %bitcast.9, bf16[4,3,256,256]{3,2,1,0:T(8,128)(2,1)S(1)} %copy-done.1, bf16[2,512,1024]{2,1,0:T(8,128)(2,1)S(1)} %copy-done.2, bf16[2,1024,512]{2,1,0:T(8,128)(2,1)S(1)} %copy-done.3), custom_call_target="tpu_custom_call" | custom-call | tf_op jit(solution)/shard_map/last_stage/pallas_call | solution.py:339
  108.8 0.0 collective-permute-done.1.received_ref
  108.8 1.0 assemble.1
  (2 shorter events, 0.0 us)
Async XLA Ops:
  4.5 7.1 %copy-start.7 = (s32[1,32,32]{2,1,0:T(8,128)S(1)}, s32[1,32,32]{2,1,0:T(8,128)}, u32[]{:S(2)}) copy-start(s32[1,32,32]{2,1,0:T(8,128)} %param.12) | copy-start | bytes 12292
  4.5 32.4 %all-to-all-start = ((bf16[32,2,16,512]{3,2,1,0:T(8,128)(2,1)}), bf16[32,2,16,512]{3,2,1,0:T(8,128)(2,1)S(1)}, u32[]{:S(2)}, u32[]{:S(2)}) async-start(bf16[32,2,16,512]{3,2,1,0:T(8,128)(2,1)} %first_graph.1), calls=%async_computation | async-start | bytes 2097152 | tf_op jit(solution)/shard_map/all_to_all | solution.py:375
  11.6 1.2 %collective-permute-start = (s32[32,32]{0,1:T(8,128)S(1)}, s32[32,32]{0,1:T(8,128)S(1)}, u32[]{:S(2)}, u32[]{:S(2)}) collective-permute-start(s32[32,32]{0,1:T(8,128)S(1)} %bitcast.15), channel_id=1, source_target_pairs={{0,1},{1,0},{2,3},{3,2},{4,5},{5,4},{6,7},{7,6},{8,9},{9,8},{10,11... | collective-permute-start | bytes 12296 | tf_op jit(solution)/shard_map/ppermute | solution.py:399
  14.5 1.2 %copy-start = (bf16[4,3,256,256]{3,2,1,0:T(8,128)(2,1)}, bf16[4,3,256,256]{3,2,1,0:T(8,128)(2,1)S(1)}, u32[]{:S(2)}) copy-start(bf16[4,3,256,256]{3,2,1,0:T(8,128)(2,1)S(1)} %spread_band.1.band_ref) | copy-start | bytes 4718596
  42.7 29.7 %copy-start.4 = (bf16[1,2,4,4,128,128]{5,4,3,2,1,0:T(8,128)(2,1)S(1)}, bf16[1,2,4,4,128,128]{5,4,3,2,1,0:T(8,128)(2,1)}, u32[]{:S(2)}) copy-start(bf16[1,2,4,4,128,128]{5,4,3,2,1,0:T(8,128)(2,1)} %values_ref.1) | copy-start | bytes 3145732
  42.7 29.7 %copy-start.5 = (s32[1,2,4,4]{3,2,1,0:T(4,128)S(1)}, s32[1,2,4,4]{3,2,1,0:T(4,128)}, u32[]{:S(2)}) copy-start(s32[1,2,4,4]{3,2,1,0:T(4,128)} %cols_ref.1) | copy-start | bytes 388
  42.7 29.7 %copy-start.6 = (s32[1,2,4]{2,1,0:T(2,128)S(1)}, s32[1,2,4]{2,1,0:T(2,128)}, u32[]{:S(2)}) copy-start(s32[1,2,4]{2,1,0:T(2,128)} %counts_ref.1) | copy-start | bytes 100
  42.7 61.3 %copy-start.3 = (bf16[2,1024,512]{2,1,0:T(8,128)(2,1)S(1)}, bf16[2,1024,512]{2,1,0:T(8,128)(2,1)}, u32[]{:S(2)}) copy-start(bf16[2,1024,512]{2,1,0:T(8,128)(2,1)} %down_ref.5) | copy-start | bytes 6291460
  72.4 31.6 %copy-start.1 = (bf16[4,3,256,256]{3,2,1,0:T(8,128)(2,1)S(1)}, bf16[4,3,256,256]{3,2,1,0:T(8,128)(2,1)}, u32[]{:S(2)}) copy-start(bf16[4,3,256,256]{3,2,1,0:T(8,128)(2,1)} %copy-done) | copy-start | bytes 4718596
  72.4 31.6 %copy-start.2 = (bf16[2,512,1024]{2,1,0:T(8,128)(2,1)S(1)}, bf16[2,512,1024]{2,1,0:T(8,128)(2,1)}, u32[]{:S(2)}) copy-start(bf16[2,512,1024]{2,1,0:T(8,128)(2,1)} %up_ref.5) | copy-start | bytes 6291460
  105.8 3.0 %collective-permute-start.1 = (bf16[32,16,512]{2,1,0:T(8,128)(2,1)S(1)}, bf16[32,16,512]{2,1,0:T(8,128)(2,1)S(1)}, u32[]{:S(2)}, u32[]{:S(2)}) collective-permute-start(bf16[32,16,512]{2,1,0:T(8,128)(2,1)S(1)} %last_stage.3), channel_id=1, source_target_pairs={{0,1},{1,0},{2,3},{3,2},{4,5},{5,4},{6,7},{7,6},{8,9},{9,8},{10,11... | collective-permute-start | bytes 1572872 | tf_op jit(solution)/shard_map/ppermute | solution.py:413

commit v2 on v1

v2 whole, which is shorter than its diff:
```python
import functools

import jax
import jax.numpy as jnp
from jax import lax
from jax.experimental import pallas as pl
from jax.experimental.pallas import tpu as pltpu
from jax.sharding import PartitionSpec as P

BAND = 32
LAYERS = 2
TILE = 256
REACH = 3
ROWS = 512
EVERY = ("snap", "span")
MIB = 1 << 20


def dot(left, right):
    return jnp.dot(left, right, preferred_element_type=jnp.float32)


def in_vmem(shape, dtype=jnp.bfloat16):
    return pltpu.VMEM(shape, dtype)


def vmem_specs(count):
    return [pl.BlockSpec(memory_space=pltpu.VMEM)] * count


def held(array):
    return pltpu.with_memory_space_constraint(array, pltpu.VMEM)


def in_hbm(array):
    return pltpu.with_memory_space_constraint(array, pltpu.HBM)


def hbm_specs(count):
    return [pl.BlockSpec(memory_space=pltpu.HBM)] * count


def params(mib=16):
    return pltpu.CompilerParams(vmem_limit_bytes=mib * MIB)


def copies(pairs, sems):
    return [pltpu.make_async_copy(*pair, sems.at[place]) for place, pair in enumerate(pairs)]


def lay_out(frame, values_ref, cols_ref, counts_ref, dense_ref):
    block_rows, slots, size, _ = values_ref.shape[1:]
    dense_ref[frame] = jnp.zeros(dense_ref.shape[1:], dense_ref.dtype)
    for row in range(block_rows):
        for slot in reversed(range(slots)):
            column = pl.multiple_of(cols_ref[frame, row, slot] * size, size)
            block = values_ref[frame, row, slot]
            used = slot < counts_ref[frame, row]
            dense_ref[frame, pl.ds(row * size, size), pl.ds(column, size)] = jnp.where(
                used, block, jnp.zeros_like(block)
            )


def propagate(frame, dense_ref, weighted, sent_ref):
    vertices = dense_ref.shape[1]
    rows = min(vertices, 512)
    own, width = sent_ref.shape[2:]
    for first in range(0, vertices, rows):
        summed = dot(dense_ref[frame, pl.ds(first, rows)], weighted).astype(jnp.bfloat16)
        sent_ref[pl.ds(first // own, rows // own), frame] = summed.reshape(
            rows // own, own, width
        )


def band_rows(coeffs, first_frame, frames_in_tile, copies_of):
    frames = coeffs.shape[0]
    back = (REACH - 1) * frames_in_tile
    lags = lax.broadcasted_iota(jnp.int32, coeffs.shape, 1)
    here = first_frame + lax.broadcasted_iota(jnp.int32, coeffs.shape, 0)
    scaled = jnp.where(here >= lags, coeffs.astype(jnp.float32), 0.0)
    weights = scaled / jnp.sum(scaled, axis=1, keepdims=True)
    sources = REACH * frames_in_tile
    place = lax.broadcasted_iota(jnp.int32, (frames, sources), 0) % frames_in_tile
    lag = back + place - lax.broadcasted_iota(jnp.int32, (frames, sources), 1)
    chosen = jnp.zeros((frames, sources), jnp.float32)
    for each in range(BAND):
        chosen = jnp.where(lag == each, weights[:, each : each + 1], chosen)
    wide = sources * copies_of
    spread = (
        lax.broadcasted_iota(jnp.int32, (sources, wide), 1) // copies_of
        == lax.broadcasted_iota(jnp.int32, (sources, wide), 0)
    ).astype(jnp.bfloat16)
    return dot(chosen.astype(jnp.bfloat16), spread)


def first_kernel(
    features_ref,
    weight_ref,
    values_ref,
    cols_ref,
    counts_ref,
    coeffs_ref,
    sent_ref,
    dense_ref,
    band_ref,
    features_in,
    weight_in,
    values_in,
    cols_in,
    counts_in,
    coeffs_in,
    sems,
):
    frames, vertices, width = features_in.shape
    loads = copies(
        [
            (coeffs_ref.at[0], coeffs_in),
            (weight_ref.at[0], weight_in),
            (features_ref.at[0], features_in),
            (cols_ref.at[0], cols_in),
            (counts_ref.at[0], counts_in),
            (values_ref.at[0], values_in),
        ],
        sems,
    )
    for load in loads:
        load.start()
    own = sent_ref.shape[2]
    loads[0].wait()
    first_frame = lax.axis_index("span") * coeffs_in.shape[0]
    band_ref[...] = band_rows(coeffs_in[...], first_frame, TILE // own, own)
    for load in loads[1:3]:
        load.wait()
    weighted = dot(features_in[...].reshape(frames * vertices, width), weight_in[...])
    weighted = weighted.astype(jnp.bfloat16).reshape(frames, vertices, width)
    for load in loads[3:]:
        load.wait()
    for frame in range(frames):
        lay_out(frame, values_in, cols_in, counts_in, dense_ref)
    for frame in range(frames):
        propagate(frame, dense_ref, weighted[frame], sent_ref)


def later_kernel(arrived_ref, dense_ref, sent_ref):
    _, frames, own, width = arrived_ref.shape
    for frame in range(frames):
        weighted = arrived_ref[:, frame].reshape(dense_ref.shape[1], width)
        propagate(frame, dense_ref, weighted, sent_ref)


def first_graph(features, weight, values, cols, counts, coeffs, owners):
    frames, vertices, width = features.shape[1:]
    own = vertices // owners
    return pl.pallas_call(
        first_kernel,
        name="first_graph",
        out_shape=[
            in_vmem((owners, frames, own, width)),
            in_vmem((frames, vertices, vertices)),
            in_vmem((coeffs.shape[1], REACH * TILE), jnp.float32),
        ],
        in_specs=hbm_specs(6),
        out_specs=vmem_specs(3),
        scratch_shapes=[
            pltpu.VMEM(features.shape[1:], jnp.bfloat16),
            pltpu.VMEM(weight.shape[1:], jnp.bfloat16),
            pltpu.VMEM(values.shape[1:], jnp.bfloat16),
            pltpu.SMEM(cols.shape[1:], jnp.int32),
            pltpu.SMEM(counts.shape[1:], jnp.int32),
            pltpu.VMEM(coeffs.shape[1:], jnp.int32),
            pltpu.SemaphoreType.DMA((6,)),
        ],
        compiler_params=params(20),
    )(*map(in_hbm, (features, weight, values, cols, counts, coeffs)))


def later_graph(arrived, dense):
    return pl.pallas_call(
        later_kernel,
        name="later_graph",
        out_shape=in_vmem(arrived.shape),
        in_specs=vmem_specs(2),
        out_specs=vmem_specs(1)[0],
        compiler_params=params(),
    )(held(arrived), held(dense))


def rows_of(ref, tile, steps):
    in_span = ref.shape[0] // steps
    first = (tile % in_span) * steps
    return (pl.ds(first, steps), tile // in_span)


def mix(place, band_tile, sources, mixed_ref, normed_ref):
    total = None
    for part, source in sources:
        term = dot(band_tile[part], source)
        total = term if total is None else total + term
    mean_square = jnp.mean(total * total, axis=-1, keepdims=True)
    rows = pl.ds(place * TILE, TILE)
    mixed_ref[rows] = total
    normed_ref[rows] = (total * lax.rsqrt(mean_square + 1e-06)).astype(jnp.bfloat16)


def perceptron(mixed_ref, normed_ref, up, down):
    active = jnp.maximum(dot(normed_ref[...], up), 0.0).astype(jnp.bfloat16)
    return (mixed_ref[...] + dot(active, down)).astype(jnp.bfloat16)


def band_tile(rows, own):
    frames, wide = rows.shape
    full = jnp.broadcast_to(rows[:, None, :], (frames, own, wide)).reshape(frames * own, wide)
    same = (
        lax.broadcasted_iota(jnp.int32, full.shape, 0) % own
        == lax.broadcasted_iota(jnp.int32, full.shape, 1) % own
    )
    return jnp.where(same, full, 0.0).astype(jnp.bfloat16)


def weight_rows(tile, in_span, mine_ref, other_ref):
    in_tile = mine_ref.shape[0] // in_span
    rows = pl.ds(tile % in_span * in_tile, in_tile)
    return jnp.where(lax.axis_index("span") == tile // in_span, mine_ref[rows], other_ref[rows])


def middle_kernel(
    layer,
    arrived_ref,
    mine_ref,
    coeffs_ref,
    up_ref,
    down_ref,
    next_ref,
    sent_ref,
    band_ref,
    other_ref,
    band_in,
    mixed_ref,
    normed_ref,
    sems,
):
    own = arrived_ref.shape[3]
    tiles, steps = band_ref.shape[0], TILE // (arrived_ref.shape[2] * own)
    width = mixed_ref.shape[1]
    together = ROWS // TILE
    in_span = tiles // arrived_ref.shape[1]
    first_frame = (1 - lax.axis_index("span")) * coeffs_ref.shape[0]
    other_ref[...] = band_rows(coeffs_ref[...], first_frame, TILE // own, own)
    for tile in range(tiles):
        full = band_tile(weight_rows(tile, in_span, mine_ref, other_ref), own)
        for source in range(REACH):
            band_in[tile, source] = full[:, source * TILE : (source + 1) * TILE]
    store = copies([(band_in, band_ref)], sems)[0]
    store.start()
    for first in range(0, tiles, together):
        for place, tile in enumerate(range(first, first + together)):
            sources = [
                (
                    REACH - 1 - back,
                    arrived_ref[rows_of(arrived_ref, tile - back, steps)].reshape(TILE, width),
                )
                for back in range(min(REACH, tile + 1))
            ]
            mix(place, band_in.at[tile], sources, mixed_ref, normed_ref)
        layer_out = perceptron(mixed_ref, normed_ref, up_ref[layer], down_ref[layer])
        result = dot(layer_out, next_ref[layer + 1]).astype(jnp.bfloat16)
        result = result.reshape(together, steps, *sent_ref.shape[2:])
        for place in range(together):
            sent_ref[rows_of(sent_ref, first + place, steps)] = result[place]
    store.wait()


def row_scratch(width):
    return [pltpu.VMEM((ROWS, width), jnp.float32), pltpu.VMEM((ROWS, width), jnp.bfloat16)]


def middle_stage(layer, arrived, mine, other_coeffs, up, down, following):
    width = up.shape[1]
    snaps, spans, frames, own, _ = arrived.shape
    band = (snaps * spans * frames * own // TILE, REACH, TILE, TILE)
    return pl.pallas_call(
        functools.partial(middle_kernel, layer),
        name="middle_stage",
        out_shape=[in_vmem(arrived.shape), pltpu.HBM(band, jnp.bfloat16)],
        in_specs=vmem_specs(6),
        out_specs=vmem_specs(1) + hbm_specs(1),
        scratch_shapes=[
            pltpu.VMEM(mine.shape, jnp.float32),
            pltpu.VMEM(band, jnp.bfloat16),
            *row_scratch(width),
            pltpu.SemaphoreType.DMA((1,)),
        ],
        compiler_params=params(24),
    )(*map(held, (arrived, mine, other_coeffs, up, down, following)))


def last_kernel(
    layer, flip, arrived_ref, band_ref, up_ref, down_ref, out_ref, mixed_ref, normed_ref
):
    span = lax.axis_index("span")
    span = 1 - span if flip else span
    steps = TILE // (arrived_ref.shape[2] * arrived_ref.shape[3])
    in_span = arrived_ref.shape[0] // steps
    width = mixed_ref.shape[1]
    own = arrived_ref.shape[3]
    frames = TILE // own
    together = ROWS // TILE
    for first in range(0, in_span, together):
        for place in range(together):
            tile = span * in_span + first + place
            sources = [
                (
                    REACH - 1 - back,
                    arrived_ref[
                        rows_of(arrived_ref, jnp.maximum(tile - back, 0), steps)
                    ].reshape(TILE, width),
                )
                for back in range(REACH)
            ]
            mix(place, band_ref.at[tile], sources, mixed_ref, normed_ref)
        layer_out = perceptron(mixed_ref, normed_ref, up_ref[layer], down_ref[layer])
        out_ref[pl.ds(first * frames, together * frames)] = layer_out.reshape(
            together * frames, own, width
        )


def last_stage(layer, flip, arrived, band, up, down):
    width = up.shape[1]
    owners, _, frames, own, _ = arrived.shape
    return pl.pallas_call(
        functools.partial(last_kernel, layer, flip),
        name="last_stage",
        out_shape=in_vmem((owners * frames, own, width)),
        in_specs=vmem_specs(4),
        out_specs=pl.BlockSpec(memory_space=pltpu.VMEM),
        scratch_shapes=row_scratch(width),
        compiler_params=params(),
    )(held(arrived), held(band), held(up), held(down))


def assemble_kernel(kept_ref, received_ref, out_ref, sems):
    span = lax.axis_index("span")
    loads = copies(
        [(kept_ref, out_ref.at[:, span]), (received_ref, out_ref.at[:, 1 - span])], sems
    )
    for load in loads:
        load.start()
    for load in loads:
        load.wait()


def assemble(kept, received):
    frames, own, width = kept.shape
    return pl.pallas_call(
        assemble_kernel,
        name="assemble",
        out_shape=pltpu.HBM((frames, 2, own, width), jnp.bfloat16),
        in_specs=vmem_specs(2),
        out_specs=hbm_specs(1)[0],
        scratch_shapes=[pltpu.SemaphoreType.DMA((2,))],
        compiler_params=params(),
    )(held(kept), held(received))


def exchange(blocks):
    return lax.all_to_all(blocks, EVERY, split_axis=0, concat_axis=0, tiled=True)


def local(
    features,
    block_values,
    block_cols,
    block_counts,
    band_coeffs,
    graph_layer_weight,
    up_weight,
    down_weight,
):
    snaps, spans = lax.axis_size("snap"), lax.axis_size("span")
    span = lax.axis_index("span")
    swap = [(0, 1), (1, 0)]
    owners = snaps * spans
    frames, vertices, width = features.shape[1:]
    own = vertices // owners
    by_owner = (snaps, spans, frames, own, width)

    other_coeffs = lax.ppermute(band_coeffs[0], "span", swap)
    sent, dense, mine = first_graph(
        features,
        graph_layer_weight,
        block_values,
        block_cols,
        block_counts,
        band_coeffs,
        owners,
    )
    sent, other_coeffs = lax.optimization_barrier((sent, other_coeffs))
    for layer in range(LAYERS - 1):
        arrived = exchange(sent).reshape(by_owner)
        sent, band = middle_stage(
            layer, arrived, mine, other_coeffs, up_weight, down_weight, graph_layer_weight
        )
        arrived = exchange(sent.reshape(owners, frames, own, width))
        sent = later_graph(arrived, dense)
    arrived = exchange(sent).reshape(by_owner)
    give = last_stage(LAYERS - 1, True, arrived, band, up_weight, down_weight)
    received = lax.ppermute(give, "span", swap)
    kept = last_stage(LAYERS - 1, False, arrived, band, up_weight, down_weight)
    return assemble(kept, received).reshape(1, snaps * frames, spans * own, width)


def solution(mesh):
    in_specs = (
        P("span", "snap", None, None),
        P("span", "snap", None, None, None, None),
        P("span", "snap", None, None),
        P("span", "snap", None),
        P("span", None, None),
        P(),
        P(),
        P(),
    )
    out_specs = P("span", None, "snap", None)
    return jax.shard_map(local, mesh=mesh, in_specs=in_specs, out_specs=out_specs, check_vma=False)
```

time: 110 us -> 107 us (0.973)
  blocking collectives: 59.3 us -> 91.9 us
  waiting for transfers between devices: 22.1 us -> 0.01 us
  starting transfers between devices: 8.57 us -> 1.3 us
  Pallas kernels: 17.9 us -> 13 us
  local copies, waits for them, and re-layouts: 1.36 us -> 0.01 us
    all_to_all x2 -> x3, blocking collectives: 59.3 us -> 91.9 us  [exchange(): lax.all_to_all(blocks, EVERY, split_axis=0, concat_axis=0, tiled=True)]
    all_to_all x1 -> x0, waiting for transfers between devices: 21.2 us -> none  [exchange(): lax.all_to_all(blocks, EVERY, split_axis=0, concat_axis=0, tiled=True)]
    all_to_all x1 -> x0, starting transfers between devices: 7.07 us -> none  [exchange(): lax.all_to_all(blocks, EVERY, split_axis=0, concat_axis=0, tiled=True)]
    pallas_call x2 -> x1, Pallas kernels: 5.63 us -> 3.3 us  [first_graph(): pl.pallas_call(first_kernel, name='first_graph', out_shape=[in_vmem((owne...]
    pallas_call x1, Pallas kernels: 5.83 us -> 4.49 us  [middle_stage(): pl.pallas_call(functools.partial(middle_kernel, layer), name='middle_stag...]
    unnamed x17 -> x8, local copies, waits for them, and re-layouts: 1.26 us -> 0.01 us
    pallas_call x1, Pallas kernels: 1.94 us -> 0.71 us  [later_graph(): pl.pallas_call(later_kernel, name='later_graph', out_shape=in_vmem(arrive...]
  transfers between devices with their start and end apart: 3 -> 2, of which waited for: 2 -> 0; matrix products, arithmetic and copies ran while one was open for 1% -> 0% of each run, Pallas kernels for 3% -> 5%
where the time goes in v2:
time: 107 us; the launch traced here: 106 us
  blocking collectives  91.9 us (86%)
  Pallas kernels  13 us (12%)
  starting transfers between devices  1.3 us (1%)
    all_to_all x3, blocking collectives, exchange(): lax.all_to_all(blocks, EVERY, split_axis=0, concat_axis=0, tiled=True)  91.9 us
    pallas_call x1, Pallas kernels, middle_stage(): pl.pallas_call(functools.partial(middle_kernel, layer), name='middle_stag...  4.49 us
    pallas_call x2, Pallas kernels, last_stage(): pl.pallas_call(functools.partial(last_kernel, layer, flip), name='last_st...  3.52 us
    pallas_call x1, Pallas kernels, first_graph(): pl.pallas_call(first_kernel, name='first_graph', out_shape=[in_vmem((owne...  3.3 us
  transfers between devices with their start and end apart: 2, of which 0 were waited for; matrix products, arithmetic and copies ran while one was open for 0% of the time, Pallas kernels for 5%

profile of v2, /device:TPU:1, one launch (start us, length us, event | category | flops | bytes accessed | tf_op | source)
XLA Modules:
  0.0 106.3 jit_solution(13854814692090915423)
XLA Ops:
  0.0 0.0 copy-start
  0.0 0.0 copy-start.1
  0.0 0.0 copy-start.3
  0.0 0.1 collective-permute-start
  0.1 3.3 %first_graph.1 = (bf16[32,2,16,512]{3,2,1,0:T(8,128)(2,1)S(1)}, bf16[2,512,512]{2,1,0:T(8,128)(2,1)S(1)}, f32[32,768]{1,0:T(8,128)S(1)}) custom-call(bf16[1,2,512,512]{3,2,1,0:T(8,128)(2,1)} %features_ref.1, bf16[2,512,512]{2,1,0:T(8,128)(2,1)} %next_ref.1, bf16[1,2,4,4,128,128]{5,4,3,2,1,0:T(8,128)(2,1)} %values_ref.1, s32[1,2,4,4]{3,2,1,0:T(4,128)} %cols_ref.1, ...), custom_call_target="tpu_custom_call" | custom-call | tf_op jit(solution)/shard_map/first_graph/pallas_call | solution.py:154
  3.4 0.0 collective-permute-done.coeffs_ref
  3.4 32.5 %all_to_all.15 = bf16[32,2,16,512]{3,2,1,0:T(8,128)(2,1)S(1)} all-to-all(bf16[32,2,16,512]{3,2,1,0:T(8,128)(2,1)S(1)} %get-tuple-element.13), channel_id=1, replica_groups=mesh['snap'=16,'span'=2] {'snap','span'}, dimensions={0} | all-to-all | bytes 2097152 | tf_op jit(solution)/shard_map/all_to_all | solution.py:366
  36.0 0.0 copy-done
  36.0 0.0 copy-done.1
  36.0 0.0 copy-done.3
  36.0 4.5 %middle_stage.1 = (bf16[16,2,2,16,512]{4,3,2,1,0:T(8,128)(2,1)S(1)}, bf16[4,3,256,256]{3,2,1,0:T(8,128)(2,1)}) custom-call(bf16[16,2,2,16,512]{4,3,2,1,0:T(8,128)(2,1)S(1)} %bitcast.7, f32[32,768]{1,0:T(8,128)S(1)} %get-tuple-element.14.mine_ref, s32[32,32]{1,0:T(8,128)S(1)} %collective-permute-done.coeffs_ref, bf16[2,512,1024]{2,1,0:T(8,128)(2,1)S(1)} %copy-done, ...), custom_call_target="tpu_custom_call" | custom-call | tf_op jit(solution)/shard_map/middle_stage/pallas_call | solution.py:281
  40.5 29.7 %all_to_all.16.arrived_ref = bf16[32,2,16,512]{3,2,1,0:T(8,128)(2,1)S(1)} all-to-all(bf16[32,2,16,512]{3,2,1,0:T(8,128)(2,1)S(1)} %bitcast.8), channel_id=1, replica_groups=mesh['snap'=16,'span'=2] {'snap','span'}, dimensions={0} | all-to-all | bytes 2097152 | tf_op jit(solution)/shard_map/all_to_all | solution.py:366
  70.1 0.0 copy-start.2
  70.1 0.7 later_graph.1
  70.8 29.7 %all_to_all.17 = bf16[32,2,16,512]{3,2,1,0:T(8,128)(2,1)S(1)} all-to-all(bf16[32,2,16,512]{3,2,1,0:T(8,128)(2,1)S(1)} %later_graph.1), channel_id=1, replica_groups=mesh['snap'=16,'span'=2] {'snap','span'}, dimensions={0} | all-to-all | bytes 2097152 | tf_op jit(solution)/shard_map/all_to_all | solution.py:366
  100.5 0.0 copy-done.2
  100.5 1.8 %last_stage.3 = bf16[32,16,512]{2,1,0:T(8,128)(2,1)S(1)} custom-call(bf16[16,2,2,16,512]{4,3,2,1,0:T(8,128)(2,1)S(1)} %bitcast.5, bf16[4,3,256,256]{3,2,1,0:T(8,128)(2,1)S(1)} %copy-done.2, bf16[2,512,1024]{2,1,0:T(8,128)(2,1)S(1)} %copy-done, bf16[2,1024,512]{2,1,0:T(8,128)(2,1)S(1)} %copy-done.1), custom_call_target="tpu_custom_call" | custom-call | tf_op jit(solution)/shard_map/last_stage/pallas_call | solution.py:330
  102.3 1.2 %collective-permute-start.1 = (bf16[32,16,512]{2,1,0:T(8,128)(2,1)S(1)}, bf16[32,16,512]{2,1,0:T(8,128)(2,1)S(1)}, u32[]{:S(2)}, u32[]{:S(2)}) collective-permute-start(bf16[32,16,512]{2,1,0:T(8,128)(2,1)S(1)} %last_stage.3), channel_id=1, source_target_pairs={{0,1},{1,0},{2,3},{3,2},{4,5},{5,4},{6,7},{7,6},{8,9},{9,8},{10,11... | collective-permute-start | bytes 1572872 | tf_op jit(solution)/shard_map/ppermute | solution.py:407
  103.5 1.8 %last_stage.2.kept_ref = bf16[32,16,512]{2,1,0:T(8,128)(2,1)S(1)} custom-call(bf16[16,2,2,16,512]{4,3,2,1,0:T(8,128)(2,1)S(1)} %bitcast.6, bf16[4,3,256,256]{3,2,1,0:T(8,128)(2,1)S(1)} %copy-done.2, bf16[2,512,1024]{2,1,0:T(8,128)(2,1)S(1)} %copy-done, bf16[2,1024,512]{2,1,0:T(8,128)(2,1)S(1)} %copy-done.1), custom_call_target="tpu_custom_call" | custom-call | tf_op jit(solution)/shard_map/last_stage/pallas_call | solution.py:330
  105.3 0.0 collective-permute-done.1.received_ref
  105.3 1.0 assemble.1
Async XLA Ops:
  0.0 36.0 %copy-start = (bf16[2,512,1024]{2,1,0:T(8,128)(2,1)S(1)}, bf16[2,512,1024]{2,1,0:T(8,128)(2,1)}, u32[]{:S(2)}) copy-start(bf16[2,512,1024]{2,1,0:T(8,128)(2,1)} %up_ref.5) | copy-start | bytes 6291460
  0.0 36.0 %copy-start.1 = (bf16[2,1024,512]{2,1,0:T(8,128)(2,1)S(1)}, bf16[2,1024,512]{2,1,0:T(8,128)(2,1)}, u32[]{:S(2)}) copy-start(bf16[2,1024,512]{2,1,0:T(8,128)(2,1)} %down_ref.5) | copy-start | bytes 6291460
  0.0 36.0 %copy-start.3 = (bf16[2,512,512]{2,1,0:T(8,128)(2,1)S(1)}, bf16[2,512,512]{2,1,0:T(8,128)(2,1)}, u32[]{:S(2)}) copy-start(bf16[2,512,512]{2,1,0:T(8,128)(2,1)} %next_ref.1) | copy-start | bytes 3145732
  0.0 3.4 %collective-permute-start = (s32[32,32]{1,0:T(8,128)}, s32[32,32]{1,0:T(8,128)S(1)}, u32[]{:S(2)}, u32[]{:S(2)}) collective-permute-start(s32[32,32]{1,0:T(8,128)} %bitcast.9), channel_id=1, source_target_pairs={{0,1},{1,0},{2,3},{3,2},{4,5},{5,4},{6,7},{7,6},{8,9},{9,8},{10,11... | collective-permute-start | bytes 12296 | tf_op jit(solution)/shard_map/ppermute | solution.py:387
  70.1 30.4 %copy-start.2 = (bf16[4,3,256,256]{3,2,1,0:T(8,128)(2,1)S(1)}, bf16[4,3,256,256]{3,2,1,0:T(8,128)(2,1)}, u32[]{:S(2)}) copy-start(bf16[4,3,256,256]{3,2,1,0:T(8,128)(2,1)} %get-tuple-element.18.band_ref) | copy-start | bytes 4718596
  102.3 3.0 %collective-permute-start.1 = (bf16[32,16,512]{2,1,0:T(8,128)(2,1)S(1)}, bf16[32,16,512]{2,1,0:T(8,128)(2,1)S(1)}, u32[]{:S(2)}, u32[]{:S(2)}) collective-permute-start(bf16[32,16,512]{2,1,0:T(8,128)(2,1)S(1)} %last_stage.3), channel_id=1, source_target_pairs={{0,1},{1,0},{2,3},{3,2},{4,5},{5,4},{6,7},{7,6},{8,9},{9,8},{10,11... | collective-permute-start | bytes 1572872 | tf_op jit(solution)/shard_map/ppermute | solution.py:407

commit v3 on v2

v3 whole, which is shorter than its diff:
```python
import functools

import jax
import jax.numpy as jnp
from jax import lax
from jax.experimental import pallas as pl
from jax.experimental.pallas import tpu as pltpu
from jax.sharding import PartitionSpec as P

BAND = 32
LAYERS = 2
TILE = 256
REACH = 3
ROWS = 512
GROUP = 16
OUTER = 4
MIB = 1 << 20


def dot(left, right):
    return jnp.dot(left, right, preferred_element_type=jnp.float32)


def in_vmem(shape, dtype=jnp.bfloat16):
    return pltpu.VMEM(shape, dtype)


def vmem_specs(count):
    return [pl.BlockSpec(memory_space=pltpu.VMEM)] * count


def held(array):
    return pltpu.with_memory_space_constraint(array, pltpu.VMEM)


def in_hbm(array):
    return pltpu.with_memory_space_constraint(array, pltpu.HBM)


def hbm_specs(count):
    return [pl.BlockSpec(memory_space=pltpu.HBM)] * count


def params(mib=16):
    return pltpu.CompilerParams(vmem_limit_bytes=mib * MIB)


def copies(pairs, sems):
    return [pltpu.make_async_copy(*pair, sems.at[place]) for place, pair in enumerate(pairs)]


def lay_out(frame, values_ref, cols_ref, counts_ref, dense_ref):
    block_rows, slots, size, _ = values_ref.shape[1:]
    dense_ref[frame] = jnp.zeros(dense_ref.shape[1:], dense_ref.dtype)
    for row in range(block_rows):
        for slot in reversed(range(slots)):
            column = pl.multiple_of(cols_ref[frame, row, slot] * size, size)
            block = values_ref[frame, row, slot]
            used = slot < counts_ref[frame, row]
            dense_ref[frame, pl.ds(row * size, size), pl.ds(column, size)] = jnp.where(
                used, block, jnp.zeros_like(block)
            )


def propagate(frame, dense_ref, weighted, sent_ref):
    vertices = dense_ref.shape[1]
    rows = min(vertices, 512)
    own, width = sent_ref.shape[2:]
    for first in range(0, vertices, rows):
        summed = dot(dense_ref[frame, pl.ds(first, rows)], weighted).astype(jnp.bfloat16)
        sent_ref[pl.ds(first // own, rows // own), frame] = summed.reshape(
            rows // own, own, width
        )


def band_rows(coeffs, first_frame, frames_in_tile, copies_of):
    frames = coeffs.shape[0]
    back = (REACH - 1) * frames_in_tile
    lags = lax.broadcasted_iota(jnp.int32, coeffs.shape, 1)
    here = first_frame + lax.broadcasted_iota(jnp.int32, coeffs.shape, 0)
    scaled = jnp.where(here >= lags, coeffs.astype(jnp.float32), 0.0)
    weights = scaled / jnp.sum(scaled, axis=1, keepdims=True)
    sources = REACH * frames_in_tile
    place = lax.broadcasted_iota(jnp.int32, (frames, sources), 0) % frames_in_tile
    lag = back + place - lax.broadcasted_iota(jnp.int32, (frames, sources), 1)
    chosen = jnp.zeros((frames, sources), jnp.float32)
    for each in range(BAND):
        chosen = jnp.where(lag == each, weights[:, each : each + 1], chosen)
    wide = sources * copies_of
    spread = (
        lax.broadcasted_iota(jnp.int32, (sources, wide), 1) // copies_of
        == lax.broadcasted_iota(jnp.int32, (sources, wide), 0)
    ).astype(jnp.bfloat16)
    return dot(chosen.astype(jnp.bfloat16), spread)


def first_kernel(
    features_ref,
    weight_ref,
    values_ref,
    cols_ref,
    counts_ref,
    coeffs_ref,
    sent_ref,
    spare_ref,
    dense_ref,
    band_ref,
    features_in,
    weight_in,
    values_in,
    cols_in,
    counts_in,
    coeffs_in,
    dense_in,
    sems,
):
    frames, vertices, width = features_in.shape
    loads = copies(
        [
            (coeffs_ref.at[0], coeffs_in),
            (weight_ref.at[0], weight_in),
            (features_ref.at[0], features_in),
            (cols_ref.at[0], cols_in),
            (counts_ref.at[0], counts_in),
            (values_ref.at[0], values_in),
        ],
        sems,
    )
    for load in loads:
        load.start()
    loads[0].wait()
    first_frame = lax.axis_index("span") * coeffs_in.shape[0]
    band_ref[...] = band_rows(coeffs_in[...], first_frame, TILE // GROUP, GROUP)
    for load in loads[1:3]:
        load.wait()
    weighted = dot(features_in[...].reshape(frames * vertices, width), weight_in[...])
    weighted = weighted.astype(jnp.bfloat16).reshape(frames, vertices, width)
    for load in loads[3:]:
        load.wait()
    for frame in range(frames):
        lay_out(frame, values_in, cols_in, counts_in, dense_in)
    store = pltpu.make_async_copy(dense_in, dense_ref, sems.at[len(loads)])
    store.start()
    for frame in range(frames):
        propagate(frame, dense_in, weighted[frame], sent_ref)
    store.wait()


def normed(mixed):
    mean_square = jnp.mean(mixed * mixed, axis=-1, keepdims=True)
    return (mixed * lax.rsqrt(mean_square + 1e-06)).astype(jnp.bfloat16)


def perceptron(mixed, up, down):
    active = jnp.maximum(dot(normed(mixed), up), 0.0).astype(jnp.bfloat16)
    return (mixed + dot(active, down)).astype(jnp.bfloat16)


def later_kernel(
    layer, mixed_ref, up_ref, down_ref, next_ref, dense_ref, sent_ref, spare_ref, weighted_ref
):
    _, frames, own, width = mixed_ref.shape
    vertices = dense_ref.shape[1]
    rows = min(vertices, 512)
    for frame in range(frames):
        for first in range(0, vertices, rows):
            mixed = mixed_ref[pl.ds(first // own, rows // own), frame].reshape(rows, width)
            layer_out = perceptron(mixed.astype(jnp.float32), up_ref[layer], down_ref[layer])
            weighted_ref[frame, pl.ds(first, rows)] = dot(
                layer_out, next_ref[layer + 1]
            ).astype(jnp.bfloat16)
    for frame in range(frames):
        propagate(frame, dense_ref, weighted_ref[frame], sent_ref)


def first_graph(features, weight, values, cols, counts, coeffs, owners):
    frames, vertices, width = features.shape[1:]
    own = vertices // owners
    large = 2 * (features.size + values.size + frames * vertices * vertices)
    return pl.pallas_call(
        first_kernel,
        name="first_graph",
        out_shape=[
            in_vmem((owners, frames, own, width)),
            pltpu.HBM((owners, frames, own, width), jnp.bfloat16),
            pltpu.HBM((frames, vertices, vertices), jnp.bfloat16),
            in_vmem((coeffs.shape[1], REACH * TILE), jnp.float32),
        ],
        in_specs=hbm_specs(6),
        out_specs=vmem_specs(1) + hbm_specs(2) + vmem_specs(1),
        scratch_shapes=[
            pltpu.VMEM(features.shape[1:], jnp.bfloat16),
            pltpu.VMEM(weight.shape[1:], jnp.bfloat16),
            pltpu.VMEM(values.shape[1:], jnp.bfloat16),
            pltpu.SMEM(cols.shape[1:], jnp.int32),
            pltpu.SMEM(counts.shape[1:], jnp.int32),
            pltpu.VMEM(coeffs.shape[1:], jnp.int32),
            pltpu.VMEM((frames, vertices, vertices), jnp.bfloat16),
            pltpu.SemaphoreType.DMA((7,)),
        ],
        compiler_params=params(17 + large // MIB),
    )(*map(in_hbm, (features, weight, values, cols, counts, coeffs)))


def later_graph(layer, mixed, up, down, following, dense):
    _, frames, _, width = mixed.shape
    return pl.pallas_call(
        functools.partial(later_kernel, layer),
        name="later_graph",
        out_shape=[in_vmem(mixed.shape), pltpu.HBM(mixed.shape, jnp.bfloat16)],
        in_specs=vmem_specs(5),
        out_specs=vmem_specs(1) + hbm_specs(1),
        scratch_shapes=[pltpu.VMEM((frames, dense.shape[1], width), jnp.bfloat16)],
        compiler_params=params(),
    )(*map(held, (mixed, up, down, following, dense)))


def band_tile(rows):
    frames, wide = rows.shape
    full = jnp.broadcast_to(rows[:, None, :], (frames, GROUP, wide)).reshape(
        frames * GROUP, wide
    )
    same = (
        lax.broadcasted_iota(jnp.int32, full.shape, 0) % GROUP
        == lax.broadcasted_iota(jnp.int32, full.shape, 1) % GROUP
    )
    return jnp.where(same, full, 0.0).astype(jnp.bfloat16)


def spread(weights_ref, band_ref):
    in_tile = TILE // GROUP
    for tile in range(band_ref.shape[0]):
        full = band_tile(weights_ref[pl.ds(tile * in_tile, in_tile)])
        for source in range(REACH):
            band_ref[tile, source] = full[:, source * TILE : (source + 1) * TILE]


def tile_index(ref, tile, group):
    steps = TILE // (GROUP * ref.shape[1])
    return (pl.ds(tile * steps, steps), slice(None), pl.ds(group * GROUP, GROUP))


def mix(tile, group, arrived_ref, halo_ref, band_ref):
    before = REACH - 1
    total = None
    for part in range(REACH):
        source = tile + part - before
        ref, source = (arrived_ref, source) if source >= 0 else (halo_ref, source + before)
        rows = ref[tile_index(ref, source, group)].reshape(TILE, ref.shape[3])
        term = dot(band_ref[tile, part], rows)
        total = term if total is None else total + term
    return total


def put(tile, group, rows, ref):
    index = tile_index(ref, tile, group)
    ref[index] = rows.reshape(index[0].size, ref.shape[1], GROUP, -1)


def gather_own(first_ref, second_ref, arrived_ref):
    for span, ref in enumerate((first_ref, second_ref)):

        @pl.when(lax.axis_index("span") == span)
        def own():
            arrived_ref[...] = ref[...]


def band_scratch(weights):
    return pltpu.VMEM((weights.shape[0] * GROUP // TILE, REACH, TILE, TILE), jnp.bfloat16)


def middle_kernel(
    first_ref, second_ref, halo_ref, weights_ref, sent_ref, arrived_ref, band_ref
):
    gather_own(first_ref, second_ref, arrived_ref)
    spread(weights_ref, band_ref)
    for group in range(arrived_ref.shape[2] // GROUP):
        for tile in range(band_ref.shape[0]):
            mixed = mix(tile, group, arrived_ref, halo_ref, band_ref)
            put(tile, group, mixed.astype(jnp.bfloat16), sent_ref)


def middle_stage(first, second, halo, weights):
    return pl.pallas_call(
        middle_kernel,
        name="middle_stage",
        out_shape=in_vmem(first.shape),
        in_specs=vmem_specs(4),
        out_specs=vmem_specs(1)[0],
        scratch_shapes=[pltpu.VMEM(first.shape, jnp.bfloat16), band_scratch(weights)],
        compiler_params=params(),
    )(*map(held, (first, second, halo, weights)))


def last_kernel(
    layer,
    first_ref,
    second_ref,
    halo_ref,
    weights_ref,
    up_ref,
    down_ref,
    out_ref,
    arrived_ref,
    out_in,
    down_in,
    band_ref,
    mixed_ref,
    sems,
):
    load = pltpu.make_async_copy(down_ref.at[layer], down_in, sems.at[0])
    load.start()
    gather_own(first_ref, second_ref, arrived_ref)
    spread(weights_ref, band_ref)
    groups = arrived_ref.shape[2] // GROUP
    places = [(slice(None), slice(None), pl.ds(group * GROUP, GROUP)) for group in range(groups)]
    stores = copies(
        [(out_in.at[place], out_ref.at[place]) for place in places], sems.at[pl.ds(1, groups)]
    )
    together = ROWS // TILE
    waited = False
    for group in range(groups):
        for first in range(0, band_ref.shape[0], together):
            tiles = range(first, first + together)
            for place, tile in enumerate(tiles):
                mixed_ref[pl.ds(place * TILE, TILE)] = mix(
                    tile, group, arrived_ref, halo_ref, band_ref
                )
            if not waited:
                load.wait()
                waited = True
            result = perceptron(mixed_ref[...], up_ref[layer], down_in[...])
            for place, tile in enumerate(tiles):
                put(tile, group, result[place * TILE : (place + 1) * TILE], out_in)
        stores[group].start()
    for store in stores:
        store.wait()


def last_stage(layer, first, second, halo, weights, up, down):
    groups = first.shape[2] // GROUP
    return pl.pallas_call(
        functools.partial(last_kernel, layer),
        name="last_stage",
        out_shape=pltpu.HBM(first.shape, jnp.bfloat16),
        in_specs=vmem_specs(5) + hbm_specs(1),
        out_specs=hbm_specs(1)[0],
        scratch_shapes=[
            pltpu.VMEM(first.shape, jnp.bfloat16),
            pltpu.VMEM(first.shape, jnp.bfloat16),
            pltpu.VMEM(down.shape[1:], jnp.bfloat16),
            band_scratch(weights),
            pltpu.VMEM((ROWS, up.shape[1]), jnp.float32),
            pltpu.SemaphoreType.DMA((1 + groups,)),
        ],
        compiler_params=params(20),
    )(*map(held, (first, second, halo, weights, up)), in_hbm(down))


def direct(blocks):
    return lax.all_to_all(blocks, "snap", split_axis=0, concat_axis=0, tiled=True)


def staged(blocks):
    count = blocks.shape[0]
    inner = count // OUTER
    runs = [list(range(first, first + inner)) for first in range(0, count, inner)]
    across = [list(range(first, count, inner)) for first in range(inner)]
    parted = blocks.reshape(OUTER, inner, *blocks.shape[1:])
    parted = lax.all_to_all(
        parted, "snap", split_axis=1, concat_axis=1, tiled=True, axis_index_groups=runs
    )
    parted = lax.all_to_all(
        parted, "snap", split_axis=0, concat_axis=0, tiled=True, axis_index_groups=across
    )
    return parted.reshape(blocks.shape)


def exchange_in_turn(blocks, spare, first_way, second_way):
    span = lax.axis_index("span")
    late = BAND // blocks.shape[1]
    first = lax.cond(
        span == 0, lambda blocks, spare: first_way(blocks), lambda blocks, spare: spare, blocks, spare
    )
    halo = lax.ppermute(first[-late:], "span", [(0, 1)])
    blocks, _ = lax.optimization_barrier((blocks, first))
    second = lax.cond(span == 0, lambda blocks: blocks, second_way, blocks)
    return first, second, halo


def local(
    features,
    block_values,
    block_cols,
    block_counts,
    band_coeffs,
    graph_layer_weight,
    up_weight,
    down_weight,
):
    snaps = lax.axis_size("snap")
    frames, vertices, width = features.shape[1:]
    sent, spare, dense, weights = first_graph(
        features,
        graph_layer_weight,
        block_values,
        block_cols,
        block_counts,
        band_coeffs,
        snaps,
    )
    for layer in range(LAYERS - 1):
        arrived = exchange_in_turn(sent, spare, direct, staged)
        mixed = direct(middle_stage(*arrived, weights))
        sent, spare = later_graph(layer, mixed, up_weight, down_weight, graph_layer_weight, dense)
    arrived = exchange_in_turn(sent, spare, direct, direct)
    out = last_stage(LAYERS - 1, *arrived, weights, up_weight, down_weight)
    return out.reshape(1, snaps * frames, vertices // snaps, width)


def solution(mesh):
    in_specs = (
        P("span", "snap", None, None),
        P("span", "snap", None, None, None, None),
        P("span", "snap", None, None),
        P("span", "snap", None),
        P("span", None, None),
        P(),
        P(),
        P(),
    )
    out_specs = P("span", None, "snap", None)
    return jax.shard_map(local, mesh=mesh, in_specs=in_specs, out_specs=out_specs, check_vma=False)
```

time: 107 us -> 98.8 us (0.923)
  blocking collectives: 91.9 us -> 79.8 us
  local copies, waits for them, and re-layouts: 0.01 us -> 1.47 us
  starting transfers between devices: 1.3 us -> 2.72 us
  Pallas kernels: 13 us -> 14.2 us
    all_to_all x3 -> x4, blocking collectives: 91.9 us -> 79.8 us  [the longest x2 40.9 us: direct(): lax.all_to_all(blocks, 'snap', split_axis=0, concat_axis=0, tiled=True)]
    ppermute x2, starting transfers between devices: 1.3 us -> 2.72 us  [exchange_in_turn(): halo = lax.ppermute(first[-late:], 'span', [(0, 1)])]
    unnamed x8 -> x12, local copies, waits for them, and re-layouts: 0.01 us -> 1.25 us
    pallas_call x5 -> x3, Pallas kernels: 9.71 us -> 10.8 us  [the longest x1 6.18 us: last_stage(): pl.pallas_call(functools.partial(last_kernel, layer), name='last_stage',...]
  transfers between devices with their start and end apart: 2 -> 2, of which waited for: 0 -> 0; matrix products, arithmetic and copies ran while one was open for 0% -> 0% of each run, Pallas kernels for 5% -> 0%
where the time goes in v3:
time: 98.8 us; the launch traced here: 98.4 us
  blocking collectives  79.8 us (81%)
  Pallas kernels  14.2 us (14%)
  starting transfers between devices  2.72 us (3%)
  local copies, waits for them, and re-layouts  1.47 us (1%)
    all_to_all x2, blocking collectives, direct(): lax.all_to_all(blocks, 'snap', split_axis=0, concat_axis=0, tiled=True)  40.9 us
    all_to_all x1, blocking collectives, staged(): lax.all_to_all(parted, 'snap', split_axis=0, concat_axis=0, tiled=True, a...  21.8 us
    all_to_all x1, blocking collectives, staged(): lax.all_to_all(parted, 'snap', split_axis=1, concat_axis=1, tiled=True, a...  17.1 us
    pallas_call x1, Pallas kernels, last_stage(): pl.pallas_call(functools.partial(last_kernel, layer), name='last_stage',...  6.18 us
    pallas_call x1, Pallas kernels, later_graph(): pl.pallas_call(functools.partial(later_kernel, layer), name='later_graph'...  3.5 us
    pallas_call x1, Pallas kernels, first_graph(): pl.pallas_call(first_kernel, name='first_graph', out_shape=[in_vmem((owne...  3.44 us
    ppermute x2, starting transfers between devices, exchange_in_turn(): halo = lax.ppermute(first[-late:], 'span', [(0, 1)])  2.72 us
  transfers between devices with their start and end apart: 2, of which 0 were waited for; matrix products, arithmetic and copies ran while one was open for 0% of the time, Pallas kernels for 0%

profile of v3, /device:TPU:1, one launch (start us, length us, event | category | flops | bytes accessed | tf_op | source)
XLA Modules:
  0.0 98.4 jit_solution(9867995684625392241)
XLA Ops:
  0.0 3.4 %first_graph.1 = (bf16[16,2,32,512]{3,2,1,0:T(8,128)(2,1)S(1)}, bf16[16,2,32,512]{3,2,1,0:T(8,128)(2,1)}, bf16[2,512,512]{2,1,0:T(8,128)(2,1)}, f32[32,768]{1,0:T(8,128)S(1)}) custom-call(bf16[1,2,512,512]{3,2,1,0:T(8,128)(2,1)} %features_ref.1, bf16[2,512,512]{2,1,0:T(8,128)(2,1)} %next_ref.1, bf16[1,2,4,4,128,128]{5,4,3,2,1,0:T(8,128)(2,1)} %values_ref.1, ...), custom_call_target="tpu_custom_call" | custom-call | tf_op jit(solution)/shard_map/first_graph/pallas_call | solution.py:180
  3.5 0.0 copy-start.4
  3.5 1.4 %collective-permute-start = (bf16[16,2,32,512]{3,2,1,0:T(8,128)(2,1)}, bf16[16,2,32,512]{3,2,1,0:T(8,128)(2,1)S(1)}, u32[]{:S(2)}, u32[]{:S(2)}) collective-permute-start(bf16[16,2,32,512]{3,2,1,0:T(8,128)(2,1)} %get-tuple-element.41.first_ref), channel_id=1, source_target_pairs={{0,1},{2,3},{4,5},{6,7},{8,9},{10,11},{12,13},{14,15},{16,17},{18,... | collective-permute-start | bytes 3145736 | tf_op jit(solution)/shard_map/ppermute | solution.py:385
  4.9 39.1 %conditional.5 = (bf16[16,2,32,512]{3,2,1,0:T(8,128)(2,1)S(1)}) conditional(s32[]{:T(128)} %convert_element_type.2, bf16[16,2,32,512]{3,2,1,0:T(8,128)(2,1)S(1)} %get-tuple-element.35, bf16[16,2,32,512]{3,2,1,0:T(8,128)(2,1)S(1)} %get-tuple-element.35), branch_computations={%region_2.0_spmd, %region_3.0_spmd} | conditional | bytes 8388616 | solution.py:387
  4.9 0.1 copy.9
  5.0 17.1 %all_to_all.26 = bf16[4,4,2,32,512]{4,3,2,0,1:T(8,128)(2,1)S(1)} all-to-all(bf16[4,4,2,32,512]{4,3,2,0,1:T(8,128)(2,1)S(1)} %copy.9), channel_id=1, replica_groups={{0,2,4,6},{8,10,12,14},{16,18,20,22},{24,26,28,30},{1,3,5,7},{9,11,13,1..., dimensions={1} | all-to-all | bytes 2097152 | tf_op jit(solution)/shard_map/cond/branch_0_fun/all_to_all | solution.py:370
  22.1 0.1 copy.10
  22.2 21.8 %all_to_all.27 = bf16[4,4,2,32,512]{4,3,2,1,0:T(8,128)(2,1)S(1)} all-to-all(bf16[4,4,2,32,512]{4,3,2,1,0:T(8,128)(2,1)S(1)} %copy.10), channel_id=1, replica_groups={{0,8,16,24},{2,10,18,26},{4,12,20,28},{6,14,22,30},{1,9,17,25},{3,11,19..., dimensions={0} | all-to-all | bytes 2097152 | tf_op jit(solution)/shard_map/cond/branch_0_fun/all_to_all | solution.py:373
  44.0 0.0 collective-permute-done.halo_ref
  44.0 0.0 copy-done.4
  44.0 0.0 copy-start.1
  44.0 0.0 copy-start.2
  44.0 0.0 copy-start.3
  44.0 1.1 %middle_stage.1 = bf16[16,2,32,512]{3,2,1,0:T(8,128)(2,1)S(1)} custom-call(bf16[16,2,32,512]{3,2,1,0:T(8,128)(2,1)S(1)} %copy-done.4, bf16[16,2,32,512]{3,2,1,0:T(8,128)(2,1)S(1)} %get-tuple-element.42.second_ref, bf16[16,2,32,512]{3,2,1,0:T(8,128)(2,1)S(1)} %collective-permute-done.halo_ref, f32[32,768]{1,0:T(8,128)S(1)} %get-tuple-element.36.weights_ref), custom_call_target="tpu_custom_call" | custom-call | tf_op jit(solution)/shard_map/middle_stage/pallas_call | solution.py:284
  45.1 0.0 copy-start
  45.1 19.4 %all_to_all.30.mixed_ref = bf16[16,2,32,512]{3,2,1,0:T(8,128)(2,1)S(1)} all-to-all(bf16[16,2,32,512]{3,2,1,0:T(8,128)(2,1)S(1)} %middle_stage.1), channel_id=1, replica_groups=mesh['snap'=16,'span'=2] {'snap'}, dimensions={0} | all-to-all | bytes 2097152 | tf_op jit(solution)/shard_map/all_to_all | solution.py:361
  64.5 0.0 copy-done.1
  64.5 0.0 copy-done.2
  64.5 0.0 copy-done.3
  64.5 0.0 copy-done
  64.5 3.5 %later_graph.1 = (bf16[16,2,32,512]{3,2,1,0:T(8,128)(2,1)S(1)}, bf16[16,2,32,512]{3,2,1,0:T(8,128)(2,1)}) custom-call(bf16[16,2,32,512]{3,2,1,0:T(8,128)(2,1)S(1)} %all_to_all.30.mixed_ref, bf16[2,512,1024]{2,1,0:T(8,128)(2,1)S(1)} %copy-done, bf16[2,1024,512]{2,1,0:T(8,128)(2,1)S(1)} %copy-done.1, bf16[2,512,512]{2,1,0:T(8,128)(2,1)S(1)} %copy-done.2, ...), custom_call_target="tpu_custom_call" | custom-call | tf_op jit(solution)/shard_map/later_graph/pallas_call | solution.py:207
  68.0 1.3 %collective-permute-start.1 = (bf16[16,2,32,512]{3,2,1,0:T(8,128)(2,1)}, bf16[16,2,32,512]{3,2,1,0:T(8,128)(2,1)}, u32[]{:S(2)}, u32[]{:S(2)}) collective-permute-start(bf16[16,2,32,512]{3,2,1,0:T(8,128)(2,1)} %get-tuple-element.43.first_ref), channel_id=1, source_target_pairs={{0,1},{2,3},{4,5},{6,7},{8,9},{10,11},{12,13},{14,15},{16,17},{18,... | collective-permute-start | bytes 3145736 | tf_op jit(solution)/shard_map/ppermute | solution.py:385
  69.3 21.7 %conditional.7 = (bf16[16,2,32,512]{3,2,1,0:T(8,128)(2,1)S(1)}) conditional(s32[]{:T(128)} %convert_element_type.2, bf16[16,2,32,512]{3,2,1,0:T(8,128)(2,1)S(1)} %get-tuple-element.40, bf16[16,2,32,512]{3,2,1,0:T(8,128)(2,1)S(1)} %get-tuple-element.40), branch_computations={%region_6.0_spmd, %region_7.0_spmd} | conditional | bytes 4194312 | solution.py:387
  69.3 0.1 copy.19
  69.4 21.6 %all_to_all.29 = bf16[16,2,32,512]{3,2,1,0:T(8,128)(2,1)S(1)} all-to-all(bf16[16,2,32,512]{3,2,1,0:T(8,128)(2,1)S(1)} %copy.19), channel_id=1, replica_groups=mesh['snap'=16,'span'=2] {'snap'}, dimensions={0} | all-to-all | bytes 2097152 | tf_op jit(solution)/shard_map/cond/branch_0_fun/all_to_all | solution.py:361
  91.0 0.0 collective-permute-done.1.halo_ref
  91.0 0.0 copy-start.5
  91.0 1.2 %copy-done.5 = bf16[16,2,32,512]{3,2,1,0:T(8,128)(2,1)S(1)} copy-done((bf16[16,2,32,512]{3,2,1,0:T(8,128)(2,1)S(1)}, bf16[16,2,32,512]{3,2,1,0:T(8,128)(2,1)}, u32[]{:S(2)}) %copy-start.5) | copy-done | bytes 1048600
  92.2 6.2 %last_stage.1 = bf16[16,2,32,512]{3,2,1,0:T(8,128)(2,1)} custom-call(bf16[16,2,32,512]{3,2,1,0:T(8,128)(2,1)S(1)} %copy-done.5, bf16[16,2,32,512]{3,2,1,0:T(8,128)(2,1)S(1)} %get-tuple-element.44.second_ref, bf16[16,2,32,512]{3,2,1,0:T(8,128)(2,1)} %collective-permute-done.1.halo_ref, f32[32,768]{1,0:T(8,128)S(1)} %get-tuple-element.36.weights_ref, ...), custom_call_target="tpu_custom_call" | custom-call | tf_op jit(solution)/shard_map/last_stage/pallas_call | solution.py:342
  (2 shorter events, 0.0 us)
Async XLA Ops:
  3.5 40.5 %copy-start.4 = (bf16[16,2,32,512]{3,2,1,0:T(8,128)(2,1)S(1)}, bf16[16,2,32,512]{3,2,1,0:T(8,128)(2,1)}, u32[]{:S(2)}) copy-start(bf16[16,2,32,512]{3,2,1,0:T(8,128)(2,1)} %get-tuple-element.41.first_ref) | copy-start | bytes 3145732
  3.5 40.5 %collective-permute-start = (bf16[16,2,32,512]{3,2,1,0:T(8,128)(2,1)}, bf16[16,2,32,512]{3,2,1,0:T(8,128)(2,1)S(1)}, u32[]{:S(2)}, u32[]{:S(2)}) collective-permute-start(bf16[16,2,32,512]{3,2,1,0:T(8,128)(2,1)} %get-tuple-element.41.first_ref), channel_id=1, source_target_pairs={{0,1},{2,3},{4,5},{6,7},{8,9},{10,11},{12,13},{14,15},{16,17},{18,... | collective-permute-start | bytes 3145736 | tf_op jit(solution)/shard_map/ppermute | solution.py:385
  44.0 20.5 %copy-start.1 = (bf16[2,1024,512]{2,1,0:T(8,128)(2,1)S(1)}, bf16[2,1024,512]{2,1,0:T(8,128)(2,1)}, u32[]{:S(2)}) copy-start(bf16[2,1024,512]{2,1,0:T(8,128)(2,1)} %down_ref.3) | copy-start | bytes 6291460
  44.0 20.5 %copy-start.2 = (bf16[2,512,512]{2,1,0:T(8,128)(2,1)S(1)}, bf16[2,512,512]{2,1,0:T(8,128)(2,1)}, u32[]{:S(2)}) copy-start(bf16[2,512,512]{2,1,0:T(8,128)(2,1)} %next_ref.1) | copy-start | bytes 3145732
  44.0 20.5 %copy-start.3 = (bf16[2,512,512]{2,1,0:T(8,128)(2,1)S(1)}, bf16[2,512,512]{2,1,0:T(8,128)(2,1)}, u32[]{:S(2)}) copy-start(bf16[2,512,512]{2,1,0:T(8,128)(2,1)} %get-tuple-element.37.dense_ref) | copy-start | bytes 3145732
  45.1 19.4 %copy-start = (bf16[2,512,1024]{2,1,0:T(8,128)(2,1)S(1)}, bf16[2,512,1024]{2,1,0:T(8,128)(2,1)}, u32[]{:S(2)}) copy-start(bf16[2,512,1024]{2,1,0:T(8,128)(2,1)} %up_ref.3) | copy-start | bytes 6291460
  68.0 23.0 %collective-permute-start.1 = (bf16[16,2,32,512]{3,2,1,0:T(8,128)(2,1)}, bf16[16,2,32,512]{3,2,1,0:T(8,128)(2,1)}, u32[]{:S(2)}, u32[]{:S(2)}) collective-permute-start(bf16[16,2,32,512]{3,2,1,0:T(8,128)(2,1)} %get-tuple-element.43.first_ref), channel_id=1, source_target_pairs={{0,1},{2,3},{4,5},{6,7},{8,9},{10,11},{12,13},{14,15},{16,17},{18,... | collective-permute-start | bytes 3145736 | tf_op jit(solution)/shard_map/ppermute | solution.py:385
  91.0 1.2 %copy-start.5 = (bf16[16,2,32,512]{3,2,1,0:T(8,128)(2,1)S(1)}, bf16[16,2,32,512]{3,2,1,0:T(8,128)(2,1)}, u32[]{:S(2)}) copy-start(bf16[16,2,32,512]{3,2,1,0:T(8,128)(2,1)} %get-tuple-element.43.first_ref) | copy-start | bytes 3145732

commit v4 on v3

--- a/solution.py
+++ b/solution.py
@@ -102,7 +102,6 @@
     counts_ref,
     coeffs_ref,
     sent_ref,
-    spare_ref,
     dense_ref,
     band_ref,
     features_in,
@@ -157,20 +156,25 @@
 
 
 def later_kernel(
-    layer, mixed_ref, up_ref, down_ref, next_ref, dense_ref, sent_ref, spare_ref, weighted_ref
+    layer, arrived_ref, up_ref, down_ref, next_ref, dense_ref, sent_ref, spare_ref, rows_ref
 ):
-    _, frames, own, width = mixed_ref.shape
+    _, frames, own, width = arrived_ref.shape
     vertices = dense_ref.shape[1]
     rows = min(vertices, 512)
     for frame in range(frames):
-        for first in range(0, vertices, rows):
-            mixed = mixed_ref[pl.ds(first // own, rows // own), frame].reshape(rows, width)
-            layer_out = perceptron(mixed.astype(jnp.float32), up_ref[layer], down_ref[layer])
-            weighted_ref[frame, pl.ds(first, rows)] = dot(
-                layer_out, next_ref[layer + 1]
-            ).astype(jnp.bfloat16)
+        rows_ref[frame] = arrived_ref[:, frame].reshape(vertices, width)
+
+    @pl.when(lax.axis_index("span") == 0)
+    def work():
+        for frame in range(frames):
+            for first in range(0, vertices, rows):
+                place = (frame, pl.ds(first, rows))
+                mixed = rows_ref[place].astype(jnp.float32)
+                rows_ref[place] = perceptron(mixed, up_ref[layer], down_ref[layer])
+
     for frame in range(frames):
-        propagate(frame, dense_ref, weighted_ref[frame], sent_ref)
+        weighted = dot(rows_ref[frame], next_ref[layer + 1]).astype(jnp.bfloat16)
+        propagate(frame, dense_ref, weighted, sent_ref)
 
 
 def first_graph(features, weight, values, cols, counts, coeffs, owners):
@@ -182,12 +186,11 @@
         name="first_graph",
         out_shape=[
             in_vmem((owners, frames, own, width)),
-            pltpu.HBM((owners, frames, own, width), jnp.bfloat16),
             pltpu.HBM((frames, vertices, vertices), jnp.bfloat16),
             in_vmem((coeffs.shape[1], REACH * TILE), jnp.float32),
         ],
         in_specs=hbm_specs(6),
-        out_specs=vmem_specs(1) + hbm_specs(2) + vmem_specs(1),
+        out_specs=vmem_specs(1) + hbm_specs(1) + vmem_specs(1),
         scratch_shapes=[
             pltpu.VMEM(features.shape[1:], jnp.bfloat16),
             pltpu.VMEM(weight.shape[1:], jnp.bfloat16),
@@ -257,12 +260,20 @@
     ref[index] = rows.reshape(index[0].size, ref.shape[1], GROUP, -1)
 
 
-def gather_own(first_ref, second_ref, arrived_ref):
+def own_load(first_ref, second_ref, arrived_ref, sem, act):
     for span, ref in enumerate((first_ref, second_ref)):
 
         @pl.when(lax.axis_index("span") == span)
         def own():
-            arrived_ref[...] = ref[...]
+            act(pltpu.make_async_copy(ref, arrived_ref, sem))
+
+
+def begin(load):
+    load.start()
+
+
+def finish(load):
+    load.wait()
 
 
 def band_scratch(weights):
@@ -270,36 +281,79 @@
 
 
 def middle_kernel(
-    first_ref, second_ref, halo_ref, weights_ref, sent_ref, arrived_ref, band_ref
+    layer,
+    halo_ref,
+    weights_ref,
+    first_ref,
+    second_ref,
+    up_ref,
+    down_ref,
+    sent_ref,
+    arrived_ref,
+    up_in,
+    down_in,
+    band_ref,
+    mixed_ref,
+    sems,
 ):
-    gather_own(first_ref, second_ref, arrived_ref)
+    second_core = lax.axis_index("span") == 1
+    loads = copies([(up_ref.at[layer], up_in), (down_ref.at[layer], down_in)], sems)
+    own_load(first_ref, second_ref, arrived_ref, sems.at[2], begin)
+
+    @pl.when(second_core)
+    def load_weights():
+        for load in loads:
+            load.start()
+
     spread(weights_ref, band_ref)
-    for group in range(arrived_ref.shape[2] // GROUP):
+    own_load(first_ref, second_ref, arrived_ref, sems.at[2], finish)
+    owners, frames, own, width = arrived_ref.shape
+    for group in range(own // GROUP):
         for tile in range(band_ref.shape[0]):
-            mixed = mix(tile, group, arrived_ref, halo_ref, band_ref)
-            put(tile, group, mixed.astype(jnp.bfloat16), sent_ref)
-
-
-def middle_stage(first, second, halo, weights):
+            put(tile, group, mix(tile, group, arrived_ref, halo_ref, band_ref), mixed_ref)
+
+    @pl.when(second_core)
+    def work():
+        for load in loads:
+            load.wait()
+        batch = ROWS // (frames * own)
+        for first in range(0, owners, batch):
+            rows = pl.ds(first, batch)
+            result = perceptron(mixed_ref[rows].reshape(ROWS, width), up_in[...], down_in[...])
+            sent_ref[rows] = result.reshape(batch, frames, own, width)
+
+    @pl.when(jnp.logical_not(second_core))
+    def leave():
+        sent_ref[...] = mixed_ref[...].astype(jnp.bfloat16)
+
+
+def middle_stage(layer, first, second, halo, weights, up, down):
     return pl.pallas_call(
-        middle_kernel,
+        functools.partial(middle_kernel, layer),
         name="middle_stage",
         out_shape=in_vmem(first.shape),
-        in_specs=vmem_specs(4),
+        in_specs=vmem_specs(2) + hbm_specs(4),
         out_specs=vmem_specs(1)[0],
-        scratch_shapes=[pltpu.VMEM(first.shape, jnp.bfloat16), band_scratch(weights)],
-        compiler_params=params(),
-    )(*map(held, (first, second, halo, weights)))
+        scratch_shapes=[
+            pltpu.VMEM(first.shape, jnp.bfloat16),
+            pltpu.VMEM(up.shape[1:], jnp.bfloat16),
+            pltpu.VMEM(down.shape[1:], jnp.bfloat16),
+            band_scratch(weights),
+            pltpu.VMEM(first.shape, jnp.float32),
+            pltpu.SemaphoreType.DMA((3,)),
+        ],
+        compiler_params=params(16 + 6 * first.size // MIB),
+    )(*map(held, (halo, weights)), *map(in_hbm, (first, second, up, down)))
 
 
 def last_kernel(
     layer,
-    first_ref,
     second_ref,
     halo_ref,
     weights_ref,
     up_ref,
     down_ref,
+    first_ref,
     out_ref,
     arrived_ref,
     out_in,
@@ -310,81 +364,111 @@
 ):
     load = pltpu.make_async_copy(down_ref.at[layer], down_in, sems.at[0])
     load.start()
-    gather_own(first_ref, second_ref, arrived_ref)
+    span = lax.axis_index("span")
+
+    @pl.when(span == 0)
+    def fetch():
+        own = pltpu.make_async_copy(first_ref, arrived_ref, sems.at[1])
+        own.start()
+        own.wait()
+
+    @pl.when(span == 1)
+    def keep():
+        arrived_ref[...] = second_ref[...]
+
     spread(weights_ref, band_ref)
-    groups = arrived_ref.shape[2] // GROUP
-    places = [(slice(None), slice(None), pl.ds(group * GROUP, GROUP)) for group in range(groups)]
-    stores = copies(
-        [(out_in.at[place], out_ref.at[place]) for place in places], sems.at[pl.ds(1, groups)]
-    )
-    together = ROWS // TILE
-    waited = False
-    for group in range(groups):
-        for first in range(0, band_ref.shape[0], together):
-            tiles = range(first, first + together)
-            for place, tile in enumerate(tiles):
-                mixed_ref[pl.ds(place * TILE, TILE)] = mix(
-                    tile, group, arrived_ref, halo_ref, band_ref
-                )
-            if not waited:
-                load.wait()
-                waited = True
-            result = perceptron(mixed_ref[...], up_ref[layer], down_in[...])
-            for place, tile in enumerate(tiles):
-                put(tile, group, result[place * TILE : (place + 1) * TILE], out_in)
-        stores[group].start()
+    owners, frames, own, width = arrived_ref.shape
+    for group in range(own // GROUP):
+        for tile in range(band_ref.shape[0]):
+            put(tile, group, mix(tile, group, arrived_ref, halo_ref, band_ref), mixed_ref)
+    load.wait()
+    batch = ROWS // (frames * own)
+    stores = []
+    for place, first in enumerate(range(0, owners, batch)):
+        rows = pl.ds(first, batch)
+        result = perceptron(
+            mixed_ref[rows].reshape(ROWS, width), up_ref[layer], down_in[...]
+        )
+        out_in[rows] = result.reshape(batch, frames, own, width)
+        store = pltpu.make_async_copy(out_in.at[rows], out_ref.at[rows], sems.at[2 + place])
+        store.start()
+        stores.append(store)
     for store in stores:
         store.wait()
 
 
 def last_stage(layer, first, second, halo, weights, up, down):
-    groups = first.shape[2] // GROUP
+    owners, frames, own, _ = first.shape
     return pl.pallas_call(
         functools.partial(last_kernel, layer),
         name="last_stage",
         out_shape=pltpu.HBM(first.shape, jnp.bfloat16),
-        in_specs=vmem_specs(5) + hbm_specs(1),
+        in_specs=vmem_specs(4) + hbm_specs(2),
         out_specs=hbm_specs(1)[0],
         scratch_shapes=[
             pltpu.VMEM(first.shape, jnp.bfloat16),
             pltpu.VMEM(first.shape, jnp.bfloat16),
             pltpu.VMEM(down.shape[1:], jnp.bfloat16),
             band_scratch(weights),
-            pltpu.VMEM((ROWS, up.shape[1]), jnp.float32),
-            pltpu.SemaphoreType.DMA((1 + groups,)),
+            pltpu.VMEM(first.shape, jnp.float32),
+            pltpu.SemaphoreType.DMA((2 + owners * frames * own // ROWS,)),
         ],
-        compiler_params=params(20),
-    )(*map(held, (first, second, halo, weights, up)), in_hbm(down))
+        compiler_params=params(16 + 8 * first.size // MIB),
+    )(*map(held, (second, halo, weights, up)), *map(in_hbm, (down, first)))
 
 
 def direct(blocks):
     return lax.all_to_all(blocks, "snap", split_axis=0, concat_axis=0, tiled=True)
 
 
-def staged(blocks):
+def runs_of(count):
+    inner = count // OUTER
+    inside = [list(range(first, first + inner)) for first in range(0, count, inner)]
+    across = [list(range(first, count, inner)) for first in range(inner)]
+    return inside, across
+
+
+def inside_runs(blocks):
     count = blocks.shape[0]
-    inner = count // OUTER
-    runs = [list(range(first, first + inner)) for first in range(0, count, inner)]
-    across = [list(range(first, count, inner)) for first in range(inner)]
-    parted = blocks.reshape(OUTER, inner, *blocks.shape[1:])
+    parted = blocks.reshape(OUTER, count // OUTER, *blocks.shape[1:])
     parted = lax.all_to_all(
-        parted, "snap", split_axis=1, concat_axis=1, tiled=True, axis_index_groups=runs
-    )
+        parted,
+        "snap",
+        split_axis=1,
+        concat_axis=1,
+        tiled=True,
+        axis_index_groups=runs_of(count)[0],
+    )
+    return parted.reshape(blocks.shape)
+
+
+def across_runs(blocks):
+    count = blocks.shape[0]
+    parted = blocks.reshape(OUTER, count // OUTER, *blocks.shape[1:])
     parted = lax.all_to_all(
-        parted, "snap", split_axis=0, concat_axis=0, tiled=True, axis_index_groups=across
+        parted,
+        "snap",
+        split_axis=0,
+        concat_axis=0,
+        tiled=True,
+        axis_index_groups=runs_of(count)[1],
     )
     return parted.reshape(blocks.shape)
 
 
-def exchange_in_turn(blocks, spare, first_way, second_way):
+def exchange_in_turn(blocks, second_begins, second_ends):
     span = lax.axis_index("span")
     late = BAND // blocks.shape[1]
-    first = lax.cond(
-        span == 0, lambda blocks, spare: first_way(blocks), lambda blocks, spare: spare, blocks, spare
-    )
+    first = lax.cond(span == 0, direct, second_begins, blocks)
     halo = lax.ppermute(first[-late:], "span", [(0, 1)])
-    blocks, _ = lax.optimization_barrier((blocks, first))
-    second = lax.cond(span == 0, lambda blocks: blocks, second_way, blocks)
+    blocks, begun = lax.optimization_barrier((blocks, first))
+    second = lax.cond(
+        span == 0,
+        lambda blocks, begun: blocks,
+        lambda blocks, begun: second_ends(blocks, begun),
+        blocks,
+        begun,
+    )
     return first, second, halo
 
 
@@ -400,7 +484,7 @@
 ):
     snaps = lax.axis_size("snap")
     frames, vertices, width = features.shape[1:]
-    sent, spare, dense, weights = first_graph(
+    sent, dense, weights = first_graph(
         features,
         graph_layer_weight,
         block_values,
@@ -410,10 +494,12 @@
         snaps,
     )
     for layer in range(LAYERS - 1):
-        arrived = exchange_in_turn(sent, spare, direct, staged)
-        mixed = direct(middle_stage(*arrived, weights))
-        sent, spare = later_graph(layer, mixed, up_weight, down_weight, graph_layer_weight, dense)
-    arrived = exchange_in_turn(sent, spare, direct, direct)
+        arrived = exchange_in_turn(sent, inside_runs, lambda blocks, begun: across_runs(begun))
+        rows = direct(middle_stage(layer, *arrived, weights, up_weight, down_weight))
+        sent, spare = later_graph(layer, rows, up_weight, down_weight, graph_layer_weight, dense)
+    arrived = exchange_in_turn(
+        sent, lambda blocks: spare, lambda blocks, begun: direct(blocks)
+    )
     out = last_stage(LAYERS - 1, *arrived, weights, up_weight, down_weight)
     return out.reshape(1, snaps * frames, vertices // snaps, width)
 

time: 98.8 us -> 95.9 us (0.971)
  blocking collectives: 79.8 us -> 75.1 us
  Pallas kernels: 14.2 us -> 15.4 us
    pallas_call x1, Pallas kernels: 1.07 us -> 4.81 us  [middle_stage(): pl.pallas_call(functools.partial(middle_kernel, layer), name='middle_stag...]
    all_to_all x2, blocking collectives: 38.9 us -> 35.7 us  [the longest x1 21.4 us: across_runs(): lax.all_to_all(parted, 'snap', split_axis=0, concat_axis=0, tiled=True, a...]
    pallas_call x1, Pallas kernels: 3.5 us -> 1.47 us  [later_graph(): pl.pallas_call(functools.partial(later_kernel, layer), name='later_graph'...]
    all_to_all x2, blocking collectives: 40.9 us -> 39.4 us  [direct(): lax.all_to_all(blocks, 'snap', split_axis=0, concat_axis=0, tiled=True)]
    all_to_all x1, local copies, waits for them, and re-layouts: 0.07 us -> 1.11 us  [inside_runs(): lax.all_to_all(parted, 'snap', split_axis=1, concat_axis=1, tiled=True, a...]
where the time goes in v4:
time: 95.9 us; the launch traced here: 95.5 us
  blocking collectives  75.1 us (78%)
  Pallas kernels  15.4 us (16%)
  starting transfers between devices  2.57 us (3%)
  local copies, waits for them, and re-layouts  2.28 us (2%)
    all_to_all x2, blocking collectives, direct(): lax.all_to_all(blocks, 'snap', split_axis=0, concat_axis=0, tiled=True)  39.4 us
    all_to_all x1, blocking collectives, across_runs(): lax.all_to_all(parted, 'snap', split_axis=0, concat_axis=0, tiled=True, a...  21.4 us
    all_to_all x1, blocking collectives, inside_runs(): lax.all_to_all(parted, 'snap', split_axis=1, concat_axis=1, tiled=True, a...  14.4 us
    pallas_call x1, Pallas kernels, last_stage(): pl.pallas_call(functools.partial(last_kernel, layer), name='last_stage',...  5.69 us
    pallas_call x1, Pallas kernels, middle_stage(): pl.pallas_call(functools.partial(middle_kernel, layer), name='middle_stag...  4.81 us
    pallas_call x1, Pallas kernels, first_graph(): pl.pallas_call(first_kernel, name='first_graph', out_shape=[in_vmem((owne...  3.44 us
    ppermute x2, starting transfers between devices, exchange_in_turn(): halo = lax.ppermute(first[-late:], 'span', [(0, 1)])  2.57 us
  transfers between devices with their start and end apart: 2, of which 0 were waited for; matrix products, arithmetic and copies ran while one was open for 0% of the time, Pallas kernels for 0%

profile of v4, /device:TPU:1, one launch (start us, length us, event | category | flops | bytes accessed | tf_op | source)
XLA Modules:
  0.0 95.5 jit_solution(10142472736902688860)
XLA Ops:
  0.0 3.4 %first_graph.1 = (bf16[16,2,32,512]{3,2,1,0:T(8,128)(2,1)S(1)}, bf16[2,512,512]{2,1,0:T(8,128)(2,1)}, f32[32,768]{1,0:T(8,128)S(1)}) custom-call(bf16[1,2,512,512]{3,2,1,0:T(8,128)(2,1)} %features_ref.1, bf16[2,512,512]{2,1,0:T(8,128)(2,1)} %next_ref.1, bf16[1,2,4,4,128,128]{5,4,3,2,1,0:T(8,128)(2,1)} %values_ref.1, s32[1,2,4,4]{3,2,1,0:T(4,128)} %cols_ref.1, ...), custom_call_target="tpu_custom_call" | custom-call | tf_op jit(solution)/shard_map/first_graph/pallas_call | solution.py:184
  3.5 15.6 %conditional.4 = (bf16[16,2,32,512]{3,2,1,0:T(8,128)(2,1)}) conditional(s32[]{:T(128)} %convert_element_type.2, bf16[16,2,32,512]{3,2,1,0:T(8,128)(2,1)S(1)} %get-tuple-element.36, bf16[16,2,32,512]{3,2,1,0:T(8,128)(2,1)S(1)} %get-tuple-element.36), branch_computations={%region_0.0_spmd, %region_1.0_spmd} | conditional | bytes 6291464 | solution.py:462
  3.5 0.1 copy.9
  3.6 14.4 %all_to_all.25 = bf16[4,4,2,32,512]{4,3,2,0,1:T(8,128)(2,1)S(1)} all-to-all(bf16[4,4,2,32,512]{4,3,2,0,1:T(8,128)(2,1)S(1)} %copy.9), channel_id=1, replica_groups={{0,2,4,6},{8,10,12,14},{16,18,20,22},{24,26,28,30},{1,3,5,7},{9,11,13,1..., dimensions={1} | all-to-all | bytes 2097152 | tf_op jit(solution)/shard_map/cond/branch_0_fun/all_to_all | solution.py:434
  18.0 1.1 %copy.10 = bf16[4,4,2,32,512]{4,3,2,1,0:T(8,128)(2,1)} copy(bf16[4,4,2,32,512]{4,3,2,0,1:T(8,128)(2,1)S(1)} %all_to_all.25) | data formatting | bytes 2097152 | tf_op jit(solution)/shard_map/cond/branch_0_fun/all_to_all | solution.py:434
  19.1 1.3 %collective-permute-start = (bf16[16,2,32,512]{3,2,1,0:T(8,128)(2,1)}, bf16[16,2,32,512]{3,2,1,0:T(8,128)(2,1)S(1)}, u32[]{:S(2)}, u32[]{:S(2)}) collective-permute-start(bf16[16,2,32,512]{3,2,1,0:T(8,128)(2,1)} %get-tuple-element.41.first_ref), channel_id=1, source_target_pairs={{0,1},{2,3},{4,5},{6,7},{8,9},{10,11},{12,13},{14,15},{16,17},{18,... | collective-permute-start | bytes 3145736 | tf_op jit(solution)/shard_map/ppermute | solution.py:463
  20.4 21.4 %conditional.5 = (bf16[16,2,32,512]{3,2,1,0:T(8,128)(2,1)S(1)}) conditional(s32[]{:T(128)} %convert_element_type.2, bf16[16,2,32,512]{3,2,1,0:T(8,128)(2,1)} %get-tuple-element.41.first_ref, bf16[16,2,32,512]{3,2,1,0:T(8,128)(2,1)S(1)} %get-tuple-element.36), branch_computations={%region_2.0_spmd, %region_3.0_spmd} | conditional | bytes 2097160 | solution.py:465
  20.4 21.4 %all_to_all.27 = bf16[4,4,2,32,512]{4,3,2,1,0:T(8,128)(2,1)S(1)} all-to-all(bf16[4,4,2,32,512]{4,3,2,1,0:T(8,128)(2,1)} %bitcast.2), channel_id=1, replica_groups={{0,8,16,24},{2,10,18,26},{4,12,20,28},{6,14,22,30},{1,9,17,25},{3,11,19..., dimensions={0} | all-to-all | bytes 2097152 | tf_op jit(solution)/shard_map/cond/branch_0_fun/all_to_all | solution.py:448
  41.7 0.0 copy-start.2
  41.7 0.0 collective-permute-done.halo_ref
  41.7 1.0 %copy-done.2 = bf16[16,2,32,512]{3,2,1,0:T(8,128)(2,1)} copy-done((bf16[16,2,32,512]{3,2,1,0:T(8,128)(2,1)}, bf16[16,2,32,512]{3,2,1,0:T(8,128)(2,1)S(1)}, u32[]{:S(2)}) %copy-start.2) | copy-done | bytes 1048600
  42.7 0.0 copy-start.1
  42.7 0.0 copy-start.3
  42.7 0.0 copy-start.4
  42.7 4.8 %middle_stage.1 = bf16[16,2,32,512]{3,2,1,0:T(8,128)(2,1)S(1)} custom-call(bf16[16,2,32,512]{3,2,1,0:T(8,128)(2,1)S(1)} %collective-permute-done.halo_ref, f32[32,768]{1,0:T(8,128)S(1)} %get-tuple-element.34.weights_ref, bf16[16,2,32,512]{3,2,1,0:T(8,128)(2,1)} %get-tuple-element.41.first_ref, bf16[16,2,32,512]{3,2,1,0:T(8,128)(2,1)} %copy-done.2, ...), custom_call_target="tpu_custom_call" | custom-call | tf_op jit(solution)/shard_map/middle_stage/pallas_call | solution.py:331
  47.5 0.0 copy-start
  47.5 19.1 %all_to_all.30.arrived_ref = bf16[16,2,32,512]{3,2,1,0:T(8,128)(2,1)S(1)} all-to-all(bf16[16,2,32,512]{3,2,1,0:T(8,128)(2,1)S(1)} %middle_stage.1), channel_id=1, replica_groups=mesh['snap'=16,'span'=2] {'snap'}, dimensions={0} | all-to-all | bytes 2097152 | tf_op jit(solution)/shard_map/all_to_all | solution.py:421
  66.7 0.0 copy-done.1
  66.7 0.0 copy-done.3
  66.7 0.0 copy-done.4
  66.7 0.0 copy-done
  66.7 1.5 %later_graph.1 = (bf16[16,2,32,512]{3,2,1,0:T(8,128)(2,1)S(1)}, bf16[16,2,32,512]{3,2,1,0:T(8,128)(2,1)}) custom-call(bf16[16,2,32,512]{3,2,1,0:T(8,128)(2,1)S(1)} %all_to_all.30.arrived_ref, bf16[2,512,1024]{2,1,0:T(8,128)(2,1)S(1)} %copy-done, bf16[2,1024,512]{2,1,0:T(8,128)(2,1)S(1)} %copy-done.1, bf16[2,512,512]{2,1,0:T(8,128)(2,1)S(1)} %copy-done.3, ...), custom_call_target="tpu_custom_call" | custom-call | tf_op jit(solution)/shard_map/later_graph/pallas_call | solution.py:210
  68.2 1.3 %collective-permute-start.1 = (bf16[16,2,32,512]{3,2,1,0:T(8,128)(2,1)}, bf16[16,2,32,512]{3,2,1,0:T(8,128)(2,1)}, u32[]{:S(2)}, u32[]{:S(2)}) collective-permute-start(bf16[16,2,32,512]{3,2,1,0:T(8,128)(2,1)} %get-tuple-element.43.first_ref), channel_id=1, source_target_pairs={{0,1},{2,3},{4,5},{6,7},{8,9},{10,11},{12,13},{14,15},{16,17},{18,... | collective-permute-start | bytes 3145736 | tf_op jit(solution)/shard_map/ppermute | solution.py:463
  69.5 20.4 %conditional.7 = (bf16[16,2,32,512]{3,2,1,0:T(8,128)(2,1)S(1)}) conditional(s32[]{:T(128)} %convert_element_type.2, bf16[16,2,32,512]{3,2,1,0:T(8,128)(2,1)S(1)} %get-tuple-element.40, bf16[16,2,32,512]{3,2,1,0:T(8,128)(2,1)S(1)} %get-tuple-element.40), branch_computations={%region_6.0_spmd, %region_7.0_spmd} | conditional | bytes 4194312 | solution.py:465
  69.5 0.1 copy.19
  69.6 20.3 %all_to_all.29 = bf16[16,2,32,512]{3,2,1,0:T(8,128)(2,1)S(1)} all-to-all(bf16[16,2,32,512]{3,2,1,0:T(8,128)(2,1)S(1)} %copy.19), channel_id=1, replica_groups=mesh['snap'=16,'span'=2] {'snap'}, dimensions={0} | all-to-all | bytes 2097152 | tf_op jit(solution)/shard_map/cond/branch_0_fun/all_to_all | solution.py:421
  89.8 0.0 collective-permute-done.1.halo_ref
  89.8 5.7 %last_stage.1 = bf16[16,2,32,512]{3,2,1,0:T(8,128)(2,1)} custom-call(bf16[16,2,32,512]{3,2,1,0:T(8,128)(2,1)S(1)} %get-tuple-element.44.second_ref, bf16[16,2,32,512]{3,2,1,0:T(8,128)(2,1)} %collective-permute-done.1.halo_ref, f32[32,768]{1,0:T(8,128)S(1)} %get-tuple-element.34.weights_ref, bf16[2,512,1024]{2,1,0:T(8,128)(2,1)S(1)} %copy-done, ...), custom_call_target="tpu_custom_call" | custom-call | tf_op jit(solution)/shard_map/last_stage/pallas_call | solution.py:402
  (1 shorter events, 0.0 us)
Async XLA Ops:
  19.1 22.7 %collective-permute-start = (bf16[16,2,32,512]{3,2,1,0:T(8,128)(2,1)}, bf16[16,2,32,512]{3,2,1,0:T(8,128)(2,1)S(1)}, u32[]{:S(2)}, u32[]{:S(2)}) collective-permute-start(bf16[16,2,32,512]{3,2,1,0:T(8,128)(2,1)} %get-tuple-element.41.first_ref), channel_id=1, source_target_pairs={{0,1},{2,3},{4,5},{6,7},{8,9},{10,11},{12,13},{14,15},{16,17},{18,... | collective-permute-start | bytes 3145736 | tf_op jit(solution)/shard_map/ppermute | solution.py:463
  41.7 1.0 %copy-start.2 = (bf16[16,2,32,512]{3,2,1,0:T(8,128)(2,1)}, bf16[16,2,32,512]{3,2,1,0:T(8,128)(2,1)S(1)}, u32[]{:S(2)}) copy-start(bf16[16,2,32,512]{3,2,1,0:T(8,128)(2,1)S(1)} %get-tuple-element.42.second_ref) | copy-start | bytes 3145732
  42.7 24.0 %copy-start.1 = (bf16[2,1024,512]{2,1,0:T(8,128)(2,1)S(1)}, bf16[2,1024,512]{2,1,0:T(8,128)(2,1)}, u32[]{:S(2)}) copy-start(bf16[2,1024,512]{2,1,0:T(8,128)(2,1)} %down_ref.5) | copy-start | bytes 6291460
  42.7 24.0 %copy-start.3 = (bf16[2,512,512]{2,1,0:T(8,128)(2,1)S(1)}, bf16[2,512,512]{2,1,0:T(8,128)(2,1)}, u32[]{:S(2)}) copy-start(bf16[2,512,512]{2,1,0:T(8,128)(2,1)} %next_ref.1) | copy-start | bytes 3145732
  42.7 24.0 %copy-start.4 = (bf16[2,512,512]{2,1,0:T(8,128)(2,1)S(1)}, bf16[2,512,512]{2,1,0:T(8,128)(2,1)}, u32[]{:S(2)}) copy-start(bf16[2,512,512]{2,1,0:T(8,128)(2,1)} %get-tuple-element.37.dense_ref) | copy-start | bytes 3145732
  47.5 19.2 %copy-start = (bf16[2,512,1024]{2,1,0:T(8,128)(2,1)S(1)}, bf16[2,512,1024]{2,1,0:T(8,128)(2,1)}, u32[]{:S(2)}) copy-start(bf16[2,512,1024]{2,1,0:T(8,128)(2,1)} %up_ref.5) | copy-start | bytes 6291460
  68.2 21.7 %collective-permute-start.1 = (bf16[16,2,32,512]{3,2,1,0:T(8,128)(2,1)}, bf16[16,2,32,512]{3,2,1,0:T(8,128)(2,1)}, u32[]{:S(2)}, u32[]{:S(2)}) collective-permute-start(bf16[16,2,32,512]{3,2,1,0:T(8,128)(2,1)} %get-tuple-element.43.first_ref), channel_id=1, source_target_pairs={{0,1},{2,3},{4,5},{6,7},{8,9},{10,11},{12,13},{14,15},{16,17},{18,... | collective-permute-start | bytes 3145736 | tf_op jit(solution)/shard_map/ppermute | solution.py:463

commit v5 on v4

--- a/solution.py
+++ b/solution.py
@@ -118,10 +118,11 @@
         [
             (coeffs_ref.at[0], coeffs_in),
             (weight_ref.at[0], weight_in),
-            (features_ref.at[0], features_in),
+            (features_ref.at[0, 0], features_in.at[0]),
             (cols_ref.at[0], cols_in),
             (counts_ref.at[0], counts_in),
             (values_ref.at[0], values_in),
+            *((features_ref.at[0, frame], features_in.at[frame]) for frame in range(1, frames)),
         ],
         sems,
     )
@@ -132,12 +133,13 @@
     band_ref[...] = band_rows(coeffs_in[...], first_frame, TILE // GROUP, GROUP)
     for load in loads[1:3]:
         load.wait()
-    weighted = dot(features_in[...].reshape(frames * vertices, width), weight_in[...])
-    weighted = weighted.astype(jnp.bfloat16).reshape(frames, vertices, width)
+    weighted = [dot(features_in[0], weight_in[...]).astype(jnp.bfloat16)]
     for load in loads[3:]:
         load.wait()
     for frame in range(frames):
         lay_out(frame, values_in, cols_in, counts_in, dense_in)
+    for frame in range(1, frames):
+        weighted.append(dot(features_in[frame], weight_in[...]).astype(jnp.bfloat16))
     store = pltpu.make_async_copy(dense_in, dense_ref, sems.at[len(loads)])
     store.start()
     for frame in range(frames):
@@ -160,17 +162,24 @@
 ):
     _, frames, own, width = arrived_ref.shape
     vertices = dense_ref.shape[1]
-    rows = min(vertices, 512)
-    for frame in range(frames):
-        rows_ref[frame] = arrived_ref[:, frame].reshape(vertices, width)
-
-    @pl.when(lax.axis_index("span") == 0)
+    batch = ROWS // (frames * own)
+    span = lax.axis_index("span")
+
+    @pl.when(span == 0)
     def work():
+        for first in range(0, arrived_ref.shape[0], batch):
+            mixed = arrived_ref[pl.ds(first, batch)].reshape(ROWS, width)
+            done = perceptron(mixed.astype(jnp.float32), up_ref[layer], down_ref[layer])
+            done = done.reshape(batch, frames, own, width)
+            for frame in range(frames):
+                rows_ref[frame, pl.ds(first * own, batch * own)] = done[:, frame].reshape(
+                    batch * own, width
+                )
+
+    @pl.when(span == 1)
+    def gather():
         for frame in range(frames):
-            for first in range(0, vertices, rows):
-                place = (frame, pl.ds(first, rows))
-                mixed = rows_ref[place].astype(jnp.float32)
-                rows_ref[place] = perceptron(mixed, up_ref[layer], down_ref[layer])
+            rows_ref[frame] = arrived_ref[:, frame].reshape(vertices, width)
 
     for frame in range(frames):
         weighted = dot(rows_ref[frame], next_ref[layer + 1]).astype(jnp.bfloat16)
@@ -199,7 +208,7 @@
             pltpu.SMEM(counts.shape[1:], jnp.int32),
             pltpu.VMEM(coeffs.shape[1:], jnp.int32),
             pltpu.VMEM((frames, vertices, vertices), jnp.bfloat16),
-            pltpu.SemaphoreType.DMA((7,)),
+            pltpu.SemaphoreType.DMA((6 + frames,)),
         ],
         compiler_params=params(17 + large // MIB),
     )(*map(in_hbm, (features, weight, values, cols, counts, coeffs)))
@@ -260,20 +269,10 @@
     ref[index] = rows.reshape(index[0].size, ref.shape[1], GROUP, -1)
 
 
-def own_load(first_ref, second_ref, arrived_ref, sem, act):
-    for span, ref in enumerate((first_ref, second_ref)):
-
-        @pl.when(lax.axis_index("span") == span)
-        def own():
-            act(pltpu.make_async_copy(ref, arrived_ref, sem))
-
-
-def begin(load):
-    load.start()
-
-
-def finish(load):
-    load.wait()
+def keep_first(first_ref, arrived_ref):
+    @pl.when(lax.axis_index("span") == 0)
+    def keep():
+        arrived_ref[...] = first_ref[...]
 
 
 def band_scratch(weights):
@@ -282,9 +281,9 @@
 
 def middle_kernel(
     layer,
+    first_ref,
     halo_ref,
     weights_ref,
-    first_ref,
     second_ref,
     up_ref,
     down_ref,
@@ -297,16 +296,27 @@
     sems,
 ):
     second_core = lax.axis_index("span") == 1
-    loads = copies([(up_ref.at[layer], up_in), (down_ref.at[layer], down_in)], sems)
-    own_load(first_ref, second_ref, arrived_ref, sems.at[2], begin)
+    loads = copies(
+        [
+            (second_ref, arrived_ref),
+            (up_ref.at[layer], up_in),
+            (down_ref.at[layer], down_in),
+        ],
+        sems,
+    )
 
     @pl.when(second_core)
-    def load_weights():
+    def load_own():
         for load in loads:
             load.start()
 
     spread(weights_ref, band_ref)
-    own_load(first_ref, second_ref, arrived_ref, sems.at[2], finish)
+    keep_first(first_ref, arrived_ref)
+
+    @pl.when(second_core)
+    def wait_own():
+        loads[0].wait()
+
     owners, frames, own, width = arrived_ref.shape
     for group in range(own // GROUP):
         for tile in range(band_ref.shape[0]):
@@ -314,7 +324,7 @@
 
     @pl.when(second_core)
     def work():
-        for load in loads:
+        for load in loads[1:]:
             load.wait()
         batch = ROWS // (frames * own)
         for first in range(0, owners, batch):
@@ -332,7 +342,7 @@
         functools.partial(middle_kernel, layer),
         name="middle_stage",
         out_shape=in_vmem(first.shape),
-        in_specs=vmem_specs(2) + hbm_specs(4),
+        in_specs=vmem_specs(3) + hbm_specs(3),
         out_specs=vmem_specs(1)[0],
         scratch_shapes=[
             pltpu.VMEM(first.shape, jnp.bfloat16),
@@ -343,7 +353,7 @@
             pltpu.SemaphoreType.DMA((3,)),
         ],
         compiler_params=params(16 + 6 * first.size // MIB),
-    )(*map(held, (halo, weights)), *map(in_hbm, (first, second, up, down)))
+    )(*map(held, (first, halo, weights)), *map(in_hbm, (second, up, down)))
 
 
 def last_kernel(

time: 95.9 us -> 94.2 us (0.982)
  local copies, waits for them, and re-layouts: 2.28 us -> 1.26 us
    all_to_all x1, local copies, waits for them, and re-layouts: 1.11 us -> 0.1 us  [inside_runs(): lax.all_to_all(parted, 'snap', split_axis=1, concat_axis=1, tiled=True, a...]
where the time goes in v5:
time: 94.2 us; the launch traced here: 93.8 us
  blocking collectives  74.6 us (79%)
  Pallas kernels  15.2 us (16%)
  starting transfers between devices  2.58 us (3%)
  local copies, waits for them, and re-layouts  1.26 us (1%)
    all_to_all x2, blocking collectives, direct(): lax.all_to_all(blocks, 'snap', split_axis=0, concat_axis=0, tiled=True)  39.1 us
    all_to_all x1, blocking collectives, across_runs(): lax.all_to_all(parted, 'snap', split_axis=0, concat_axis=0, tiled=True, a...  21.2 us
    all_to_all x1, blocking collectives, inside_runs(): lax.all_to_all(parted, 'snap', split_axis=1, concat_axis=1, tiled=True, a...  14.3 us
    pallas_call x1, Pallas kernels, last_stage(): pl.pallas_call(functools.partial(last_kernel, layer), name='last_stage',...  5.69 us
    pallas_call x1, Pallas kernels, middle_stage(): pl.pallas_call(functools.partial(middle_kernel, layer), name='middle_stag...  4.8 us
    pallas_call x1, Pallas kernels, first_graph(): pl.pallas_call(first_kernel, name='first_graph', out_shape=[in_vmem((owne...  3.23 us
    ppermute x2, starting transfers between devices, exchange_in_turn(): halo = lax.ppermute(first[-late:], 'span', [(0, 1)])  2.58 us
  transfers between devices with their start and end apart: 2, of which 0 were waited for; matrix products, arithmetic and copies ran while one was open for 0% of the time, Pallas kernels for 0%

profile of v5, /device:TPU:1, one launch (start us, length us, event | category | flops | bytes accessed | tf_op | source)
XLA Modules:
  0.0 93.8 jit_solution(15517504243890917184)
XLA Ops:
  0.0 3.2 %first_graph.1 = (bf16[16,2,32,512]{3,2,1,0:T(8,128)(2,1)S(1)}, bf16[2,512,512]{2,1,0:T(8,128)(2,1)}, f32[32,768]{1,0:T(8,128)S(1)}) custom-call(bf16[1,2,512,512]{3,2,1,0:T(8,128)(2,1)} %features_ref.1, bf16[2,512,512]{2,1,0:T(8,128)(2,1)} %next_ref.1, bf16[1,2,4,4,128,128]{5,4,3,2,1,0:T(8,128)(2,1)} %values_ref.1, s32[1,2,4,4]{3,2,1,0:T(4,128)} %cols_ref.1, ...), custom_call_target="tpu_custom_call" | custom-call | tf_op jit(solution)/shard_map/first_graph/pallas_call | solution.py:193
  3.2 14.5 %conditional.4 = (bf16[16,2,32,512]{3,2,1,0:T(8,128)(2,1)S(1)}) conditional(s32[]{:T(128)} %convert_element_type.2, bf16[16,2,32,512]{3,2,1,0:T(8,128)(2,1)S(1)} %get-tuple-element.36, bf16[16,2,32,512]{3,2,1,0:T(8,128)(2,1)S(1)} %get-tuple-element.36), branch_computations={%region_0.0_spmd, %region_1.0_spmd} | conditional | bytes 6291464 | solution.py:472
  3.3 0.1 copy.9
  3.4 14.3 %all_to_all.25 = bf16[4,4,2,32,512]{4,3,2,0,1:T(8,128)(2,1)S(1)} all-to-all(bf16[4,4,2,32,512]{4,3,2,0,1:T(8,128)(2,1)S(1)} %copy.9), channel_id=1, replica_groups={{0,2,4,6},{8,10,12,14},{16,18,20,22},{24,26,28,30},{1,3,5,7},{9,11,13,1..., dimensions={1} | all-to-all | bytes 2097152 | tf_op jit(solution)/shard_map/cond/branch_0_fun/all_to_all | solution.py:444
  17.6 0.1 copy.10
  17.8 1.3 %collective-permute-start = (bf16[16,2,32,512]{3,2,1,0:T(8,128)(2,1)S(1)}, bf16[16,2,32,512]{3,2,1,0:T(8,128)(2,1)S(1)}, u32[]{:S(2)}, u32[]{:S(2)}) collective-permute-start(bf16[16,2,32,512]{3,2,1,0:T(8,128)(2,1)S(1)} %get-tuple-element.41.first_ref), channel_id=1, source_target_pairs={{0,1},{2,3},{4,5},{6,7},{8,9},{10,11},{12,13},{14,15},{16,17},{18,... | collective-permute-start | bytes 3145736 | tf_op jit(solution)/shard_map/ppermute | solution.py:473
  19.1 21.2 %conditional.5 = (bf16[16,2,32,512]{3,2,1,0:T(8,128)(2,1)S(1)}) conditional(s32[]{:T(128)} %convert_element_type.2, bf16[16,2,32,512]{3,2,1,0:T(8,128)(2,1)S(1)} %get-tuple-element.41.first_ref, bf16[16,2,32,512]{3,2,1,0:T(8,128)(2,1)S(1)} %get-tuple-element.36), branch_computations={%region_2.0_spmd, %region_3.0_spmd} | conditional | bytes 2097160 | solution.py:475
  19.1 21.2 %all_to_all.27 = bf16[4,4,2,32,512]{4,3,2,1,0:T(8,128)(2,1)S(1)} all-to-all(bf16[4,4,2,32,512]{4,3,2,1,0:T(8,128)(2,1)S(1)} %bitcast.8), channel_id=1, replica_groups={{0,8,16,24},{2,10,18,26},{4,12,20,28},{6,14,22,30},{1,9,17,25},{3,11,19..., dimensions={0} | all-to-all | bytes 2097152 | tf_op jit(solution)/shard_map/cond/branch_0_fun/all_to_all | solution.py:458
  40.3 0.0 copy-start.2
  40.3 0.0 collective-permute-done.halo_ref
  40.3 1.0 %copy-done.2 = bf16[16,2,32,512]{3,2,1,0:T(8,128)(2,1)} copy-done((bf16[16,2,32,512]{3,2,1,0:T(8,128)(2,1)}, bf16[16,2,32,512]{3,2,1,0:T(8,128)(2,1)S(1)}, u32[]{:S(2)}) %copy-start.2) | copy-done | bytes 1048600
  41.3 0.0 copy-start.1
  41.3 0.0 copy-start.3
  41.3 0.0 copy-start.4
  41.3 4.8 %middle_stage.1 = bf16[16,2,32,512]{3,2,1,0:T(8,128)(2,1)S(1)} custom-call(bf16[16,2,32,512]{3,2,1,0:T(8,128)(2,1)S(1)} %get-tuple-element.41.first_ref, bf16[16,2,32,512]{3,2,1,0:T(8,128)(2,1)S(1)} %collective-permute-done.halo_ref, f32[32,768]{1,0:T(8,128)S(1)} %get-tuple-element.34.weights_ref, bf16[16,2,32,512]{3,2,1,0:T(8,128)(2,1)} %copy-done.2, ...), custom_call_target="tpu_custom_call" | custom-call | tf_op jit(solution)/shard_map/middle_stage/pallas_call | solution.py:341
  46.1 0.0 copy-start
  46.1 19.2 %all_to_all.30.arrived_ref = bf16[16,2,32,512]{3,2,1,0:T(8,128)(2,1)S(1)} all-to-all(bf16[16,2,32,512]{3,2,1,0:T(8,128)(2,1)S(1)} %middle_stage.1), channel_id=1, replica_groups=mesh['snap'=16,'span'=2] {'snap'}, dimensions={0} | all-to-all | bytes 2097152 | tf_op jit(solution)/shard_map/all_to_all | solution.py:431
  65.3 0.0 copy-done.1
  65.3 0.0 copy-done.3
  65.3 0.0 copy-done.4
  65.3 0.0 copy-done
  65.3 1.5 %later_graph.1 = (bf16[16,2,32,512]{3,2,1,0:T(8,128)(2,1)S(1)}, bf16[16,2,32,512]{3,2,1,0:T(8,128)(2,1)}) custom-call(bf16[16,2,32,512]{3,2,1,0:T(8,128)(2,1)S(1)} %all_to_all.30.arrived_ref, bf16[2,512,1024]{2,1,0:T(8,128)(2,1)S(1)} %copy-done, bf16[2,1024,512]{2,1,0:T(8,128)(2,1)S(1)} %copy-done.1, bf16[2,512,512]{2,1,0:T(8,128)(2,1)S(1)} %copy-done.3, ...), custom_call_target="tpu_custom_call" | custom-call | tf_op jit(solution)/shard_map/later_graph/pallas_call | solution.py:219
  66.8 1.3 %collective-permute-start.1 = (bf16[16,2,32,512]{3,2,1,0:T(8,128)(2,1)}, bf16[16,2,32,512]{3,2,1,0:T(8,128)(2,1)}, u32[]{:S(2)}, u32[]{:S(2)}) collective-permute-start(bf16[16,2,32,512]{3,2,1,0:T(8,128)(2,1)} %get-tuple-element.43.first_ref), channel_id=1, source_target_pairs={{0,1},{2,3},{4,5},{6,7},{8,9},{10,11},{12,13},{14,15},{16,17},{18,... | collective-permute-start | bytes 3145736 | tf_op jit(solution)/shard_map/ppermute | solution.py:473
  68.1 20.0 %conditional.7 = (bf16[16,2,32,512]{3,2,1,0:T(8,128)(2,1)S(1)}) conditional(s32[]{:T(128)} %convert_element_type.2, bf16[16,2,32,512]{3,2,1,0:T(8,128)(2,1)S(1)} %get-tuple-element.40, bf16[16,2,32,512]{3,2,1,0:T(8,128)(2,1)S(1)} %get-tuple-element.40), branch_computations={%region_6.0_spmd, %region_7.0_spmd} | conditional | bytes 4194312 | solution.py:475
  68.1 0.1 copy.19
  68.2 19.9 %all_to_all.29 = bf16[16,2,32,512]{3,2,1,0:T(8,128)(2,1)S(1)} all-to-all(bf16[16,2,32,512]{3,2,1,0:T(8,128)(2,1)S(1)} %copy.19), channel_id=1, replica_groups=mesh['snap'=16,'span'=2] {'snap'}, dimensions={0} | all-to-all | bytes 2097152 | tf_op jit(solution)/shard_map/cond/branch_0_fun/all_to_all | solution.py:431
  88.1 0.0 collective-permute-done.1.halo_ref
  88.1 5.7 %last_stage.1 = bf16[16,2,32,512]{3,2,1,0:T(8,128)(2,1)} custom-call(bf16[16,2,32,512]{3,2,1,0:T(8,128)(2,1)S(1)} %get-tuple-element.44.second_ref, bf16[16,2,32,512]{3,2,1,0:T(8,128)(2,1)} %collective-permute-done.1.halo_ref, f32[32,768]{1,0:T(8,128)S(1)} %get-tuple-element.34.weights_ref, bf16[2,512,1024]{2,1,0:T(8,128)(2,1)S(1)} %copy-done, ...), custom_call_target="tpu_custom_call" | custom-call | tf_op jit(solution)/shard_map/last_stage/pallas_call | solution.py:412
  (1 shorter events, 0.0 us)
Async XLA Ops:
  17.8 22.5 %collective-permute-start = (bf16[16,2,32,512]{3,2,1,0:T(8,128)(2,1)S(1)}, bf16[16,2,32,512]{3,2,1,0:T(8,128)(2,1)S(1)}, u32[]{:S(2)}, u32[]{:S(2)}) collective-permute-start(bf16[16,2,32,512]{3,2,1,0:T(8,128)(2,1)S(1)} %get-tuple-element.41.first_ref), channel_id=1, source_target_pairs={{0,1},{2,3},{4,5},{6,7},{8,9},{10,11},{12,13},{14,15},{16,17},{18,... | collective-permute-start | bytes 3145736 | tf_op jit(solution)/shard_map/ppermute | solution.py:473
  40.3 1.0 %copy-start.2 = (bf16[16,2,32,512]{3,2,1,0:T(8,128)(2,1)}, bf16[16,2,32,512]{3,2,1,0:T(8,128)(2,1)S(1)}, u32[]{:S(2)}) copy-start(bf16[16,2,32,512]{3,2,1,0:T(8,128)(2,1)S(1)} %get-tuple-element.42.second_ref) | copy-start | bytes 3145732
  41.3 24.0 %copy-start.1 = (bf16[2,1024,512]{2,1,0:T(8,128)(2,1)S(1)}, bf16[2,1024,512]{2,1,0:T(8,128)(2,1)}, u32[]{:S(2)}) copy-start(bf16[2,1024,512]{2,1,0:T(8,128)(2,1)} %down_ref.5) | copy-start | bytes 6291460
  41.3 24.0 %copy-start.3 = (bf16[2,512,512]{2,1,0:T(8,128)(2,1)S(1)}, bf16[2,512,512]{2,1,0:T(8,128)(2,1)}, u32[]{:S(2)}) copy-start(bf16[2,512,512]{2,1,0:T(8,128)(2,1)} %next_ref.1) | copy-start | bytes 3145732
  41.3 24.0 %copy-start.4 = (bf16[2,512,512]{2,1,0:T(8,128)(2,1)S(1)}, bf16[2,512,512]{2,1,0:T(8,128)(2,1)}, u32[]{:S(2)}) copy-start(bf16[2,512,512]{2,1,0:T(8,128)(2,1)} %get-tuple-element.37.dense_ref) | copy-start | bytes 3145732
  46.1 19.2 %copy-start = (bf16[2,512,1024]{2,1,0:T(8,128)(2,1)S(1)}, bf16[2,512,1024]{2,1,0:T(8,128)(2,1)}, u32[]{:S(2)}) copy-start(bf16[2,512,1024]{2,1,0:T(8,128)(2,1)} %up_ref.5) | copy-start | bytes 6291460
  66.8 21.3 %collective-permute-start.1 = (bf16[16,2,32,512]{3,2,1,0:T(8,128)(2,1)}, bf16[16,2,32,512]{3,2,1,0:T(8,128)(2,1)}, u32[]{:S(2)}, u32[]{:S(2)}) collective-permute-start(bf16[16,2,32,512]{3,2,1,0:T(8,128)(2,1)} %get-tuple-element.43.first_ref), channel_id=1, source_target_pairs={{0,1},{2,3},{4,5},{6,7},{8,9},{10,11},{12,13},{14,15},{16,17},{18,... | collective-permute-start | bytes 3145736 | tf_op jit(solution)/shard_map/ppermute | solution.py:473

commit v6 on v5

--- a/solution.py
+++ b/solution.py
@@ -181,9 +181,10 @@
         for frame in range(frames):
             rows_ref[frame] = arrived_ref[:, frame].reshape(vertices, width)
 
+    weighted = dot(rows_ref[...].reshape(frames * vertices, width), next_ref[layer + 1])
+    weighted = weighted.astype(jnp.bfloat16).reshape(frames, vertices, width)
     for frame in range(frames):
-        weighted = dot(rows_ref[frame], next_ref[layer + 1]).astype(jnp.bfloat16)
-        propagate(frame, dense_ref, weighted, sent_ref)
+        propagate(frame, dense_ref, weighted[frame], sent_ref)
 
 
 def first_graph(features, weight, values, cols, counts, coeffs, owners):
@@ -393,13 +394,14 @@
             put(tile, group, mix(tile, group, arrived_ref, halo_ref, band_ref), mixed_ref)
     load.wait()
     batch = ROWS // (frames * own)
+    parts = [(first, batch) for first in range(0, owners - batch, batch)]
+    parts += [(owners - batch, batch // 2), (owners - batch // 2, batch // 2)]
     stores = []
-    for place, first in enumerate(range(0, owners, batch)):
-        rows = pl.ds(first, batch)
-        result = perceptron(
-            mixed_ref[rows].reshape(ROWS, width), up_ref[layer], down_in[...]
-        )
-        out_in[rows] = result.reshape(batch, frames, own, width)
+    for place, (first, count) in enumerate(parts):
+        rows = pl.ds(first, count)
+        mixed = mixed_ref[rows].reshape(count * frames * own, width)
+        result = perceptron(mixed, up_ref[layer], down_in[...])
+        out_in[rows] = result.reshape(count, frames, own, width)
         store = pltpu.make_async_copy(out_in.at[rows], out_ref.at[rows], sems.at[2 + place])
         store.start()
         stores.append(store)
@@ -421,7 +423,7 @@
             pltpu.VMEM(down.shape[1:], jnp.bfloat16),
             band_scratch(weights),
             pltpu.VMEM(first.shape, jnp.float32),
-            pltpu.SemaphoreType.DMA((2 + owners * frames * own // ROWS,)),
+            pltpu.SemaphoreType.DMA((3 + owners * frames * own // ROWS,)),
         ],
         compiler_params=params(16 + 8 * first.size // MIB),
     )(*map(held, (second, halo, weights, up)), *map(in_hbm, (down, first)))

time: 94.2 us -> 93.9 us (level)
  no operation moved by 1% of the time
where the time goes in v6:
time: 93.9 us; the launch traced here: 93.6 us
  blocking collectives  74.6 us (79%)
  Pallas kernels  15 us (16%)
  starting transfers between devices  2.58 us (3%)
  local copies, waits for them, and re-layouts  1.26 us (1%)
    all_to_all x2, blocking collectives, direct(): lax.all_to_all(blocks, 'snap', split_axis=0, concat_axis=0, tiled=True)  39.1 us
    all_to_all x1, blocking collectives, across_runs(): lax.all_to_all(parted, 'snap', split_axis=0, concat_axis=0, tiled=True, a...  21.2 us
    all_to_all x1, blocking collectives, inside_runs(): lax.all_to_all(parted, 'snap', split_axis=1, concat_axis=1, tiled=True, a...  14.3 us
    pallas_call x1, Pallas kernels, last_stage(): pl.pallas_call(functools.partial(last_kernel, layer), name='last_stage',...  5.61 us
    pallas_call x1, Pallas kernels, middle_stage(): pl.pallas_call(functools.partial(middle_kernel, layer), name='middle_stag...  4.81 us
    pallas_call x1, Pallas kernels, first_graph(): pl.pallas_call(first_kernel, name='first_graph', out_shape=[in_vmem((owne...  3.23 us
    ppermute x2, starting transfers between devices, exchange_in_turn(): halo = lax.ppermute(first[-late:], 'span', [(0, 1)])  2.58 us
  transfers between devices with their start and end apart: 2, of which 0 were waited for; matrix products, arithmetic and copies ran while one was open for 0% of the time, Pallas kernels for 0%

profile of v6, /device:TPU:1, one launch (start us, length us, event | category | flops | bytes accessed | tf_op | source)
XLA Modules:
  0.0 93.6 jit_solution(5938027669650137801)
XLA Ops:
  0.0 3.2 %first_graph.1 = (bf16[16,2,32,512]{3,2,1,0:T(8,128)(2,1)S(1)}, bf16[2,512,512]{2,1,0:T(8,128)(2,1)}, f32[32,768]{1,0:T(8,128)S(1)}) custom-call(bf16[1,2,512,512]{3,2,1,0:T(8,128)(2,1)} %features_ref.1, bf16[2,512,512]{2,1,0:T(8,128)(2,1)} %next_ref.1, bf16[1,2,4,4,128,128]{5,4,3,2,1,0:T(8,128)(2,1)} %values_ref.1, s32[1,2,4,4]{3,2,1,0:T(4,128)} %cols_ref.1, ...), custom_call_target="tpu_custom_call" | custom-call | tf_op jit(solution)/shard_map/first_graph/pallas_call | solution.py:194
  3.2 14.5 %conditional.4 = (bf16[16,2,32,512]{3,2,1,0:T(8,128)(2,1)S(1)}) conditional(s32[]{:T(128)} %convert_element_type.2, bf16[16,2,32,512]{3,2,1,0:T(8,128)(2,1)S(1)} %get-tuple-element.36, bf16[16,2,32,512]{3,2,1,0:T(8,128)(2,1)S(1)} %get-tuple-element.36), branch_computations={%region_0.0_spmd, %region_1.0_spmd} | conditional | bytes 6291464 | solution.py:474
  3.2 0.1 copy.9
  3.4 14.3 %all_to_all.25 = bf16[4,4,2,32,512]{4,3,2,0,1:T(8,128)(2,1)S(1)} all-to-all(bf16[4,4,2,32,512]{4,3,2,0,1:T(8,128)(2,1)S(1)} %copy.9), channel_id=1, replica_groups={{0,2,4,6},{8,10,12,14},{16,18,20,22},{24,26,28,30},{1,3,5,7},{9,11,13,1..., dimensions={1} | all-to-all | bytes 2097152 | tf_op jit(solution)/shard_map/cond/branch_0_fun/all_to_all | solution.py:446
  17.6 0.1 copy.10
  17.8 1.3 %collective-permute-start = (bf16[16,2,32,512]{3,2,1,0:T(8,128)(2,1)S(1)}, bf16[16,2,32,512]{3,2,1,0:T(8,128)(2,1)S(1)}, u32[]{:S(2)}, u32[]{:S(2)}) collective-permute-start(bf16[16,2,32,512]{3,2,1,0:T(8,128)(2,1)S(1)} %get-tuple-element.41.first_ref), channel_id=1, source_target_pairs={{0,1},{2,3},{4,5},{6,7},{8,9},{10,11},{12,13},{14,15},{16,17},{18,... | collective-permute-start | bytes 3145736 | tf_op jit(solution)/shard_map/ppermute | solution.py:475
  19.1 21.2 %conditional.5 = (bf16[16,2,32,512]{3,2,1,0:T(8,128)(2,1)S(1)}) conditional(s32[]{:T(128)} %convert_element_type.2, bf16[16,2,32,512]{3,2,1,0:T(8,128)(2,1)S(1)} %get-tuple-element.41.first_ref, bf16[16,2,32,512]{3,2,1,0:T(8,128)(2,1)S(1)} %get-tuple-element.36), branch_computations={%region_2.0_spmd, %region_3.0_spmd} | conditional | bytes 2097160 | solution.py:477
  19.1 21.2 %all_to_all.27 = bf16[4,4,2,32,512]{4,3,2,1,0:T(8,128)(2,1)S(1)} all-to-all(bf16[4,4,2,32,512]{4,3,2,1,0:T(8,128)(2,1)S(1)} %bitcast.8), channel_id=1, replica_groups={{0,8,16,24},{2,10,18,26},{4,12,20,28},{6,14,22,30},{1,9,17,25},{3,11,19..., dimensions={0} | all-to-all | bytes 2097152 | tf_op jit(solution)/shard_map/cond/branch_0_fun/all_to_all | solution.py:460
  40.3 0.0 copy-start.2
  40.3 0.0 collective-permute-done.halo_ref
  40.3 1.0 %copy-done.2 = bf16[16,2,32,512]{3,2,1,0:T(8,128)(2,1)} copy-done((bf16[16,2,32,512]{3,2,1,0:T(8,128)(2,1)}, bf16[16,2,32,512]{3,2,1,0:T(8,128)(2,1)S(1)}, u32[]{:S(2)}) %copy-start.2) | copy-done | bytes 1048600
  41.3 0.0 copy-start.1
  41.3 0.0 copy-start.3
  41.3 0.0 copy-start.4
  41.3 4.8 %middle_stage.1 = bf16[16,2,32,512]{3,2,1,0:T(8,128)(2,1)S(1)} custom-call(bf16[16,2,32,512]{3,2,1,0:T(8,128)(2,1)S(1)} %get-tuple-element.41.first_ref, bf16[16,2,32,512]{3,2,1,0:T(8,128)(2,1)S(1)} %collective-permute-done.halo_ref, f32[32,768]{1,0:T(8,128)S(1)} %get-tuple-element.34.weights_ref, bf16[16,2,32,512]{3,2,1,0:T(8,128)(2,1)} %copy-done.2, ...), custom_call_target="tpu_custom_call" | custom-call | tf_op jit(solution)/shard_map/middle_stage/pallas_call | solution.py:342
  46.1 0.0 copy-start
  46.1 19.4 %all_to_all.30.arrived_ref = bf16[16,2,32,512]{3,2,1,0:T(8,128)(2,1)S(1)} all-to-all(bf16[16,2,32,512]{3,2,1,0:T(8,128)(2,1)S(1)} %middle_stage.1), channel_id=1, replica_groups=mesh['snap'=16,'span'=2] {'snap'}, dimensions={0} | all-to-all | bytes 2097152 | tf_op jit(solution)/shard_map/all_to_all | solution.py:433
  65.5 0.0 copy-done.1
  65.5 0.0 copy-done.3
  65.5 0.0 copy-done.4
  65.5 0.0 copy-done
  65.5 1.3 %later_graph.1 = (bf16[16,2,32,512]{3,2,1,0:T(8,128)(2,1)S(1)}, bf16[16,2,32,512]{3,2,1,0:T(8,128)(2,1)}) custom-call(bf16[16,2,32,512]{3,2,1,0:T(8,128)(2,1)S(1)} %all_to_all.30.arrived_ref, bf16[2,512,1024]{2,1,0:T(8,128)(2,1)S(1)} %copy-done, bf16[2,1024,512]{2,1,0:T(8,128)(2,1)S(1)} %copy-done.1, bf16[2,512,512]{2,1,0:T(8,128)(2,1)S(1)} %copy-done.3, ...), custom_call_target="tpu_custom_call" | custom-call | tf_op jit(solution)/shard_map/later_graph/pallas_call | solution.py:220
  66.9 1.3 %collective-permute-start.1 = (bf16[16,2,32,512]{3,2,1,0:T(8,128)(2,1)}, bf16[16,2,32,512]{3,2,1,0:T(8,128)(2,1)}, u32[]{:S(2)}, u32[]{:S(2)}) collective-permute-start(bf16[16,2,32,512]{3,2,1,0:T(8,128)(2,1)} %get-tuple-element.43.first_ref), channel_id=1, source_target_pairs={{0,1},{2,3},{4,5},{6,7},{8,9},{10,11},{12,13},{14,15},{16,17},{18,... | collective-permute-start | bytes 3145736 | tf_op jit(solution)/shard_map/ppermute | solution.py:475
  68.2 19.8 %conditional.7 = (bf16[16,2,32,512]{3,2,1,0:T(8,128)(2,1)S(1)}) conditional(s32[]{:T(128)} %convert_element_type.2, bf16[16,2,32,512]{3,2,1,0:T(8,128)(2,1)S(1)} %get-tuple-element.40, bf16[16,2,32,512]{3,2,1,0:T(8,128)(2,1)S(1)} %get-tuple-element.40), branch_computations={%region_6.0_spmd, %region_7.0_spmd} | conditional | bytes 4194312 | solution.py:477
  68.2 0.1 copy.19
  68.3 19.7 %all_to_all.29 = bf16[16,2,32,512]{3,2,1,0:T(8,128)(2,1)S(1)} all-to-all(bf16[16,2,32,512]{3,2,1,0:T(8,128)(2,1)S(1)} %copy.19), channel_id=1, replica_groups=mesh['snap'=16,'span'=2] {'snap'}, dimensions={0} | all-to-all | bytes 2097152 | tf_op jit(solution)/shard_map/cond/branch_0_fun/all_to_all | solution.py:433
  87.9 0.0 collective-permute-done.1.halo_ref
  88.0 5.6 %last_stage.1 = bf16[16,2,32,512]{3,2,1,0:T(8,128)(2,1)} custom-call(bf16[16,2,32,512]{3,2,1,0:T(8,128)(2,1)S(1)} %get-tuple-element.44.second_ref, bf16[16,2,32,512]{3,2,1,0:T(8,128)(2,1)} %collective-permute-done.1.halo_ref, f32[32,768]{1,0:T(8,128)S(1)} %get-tuple-element.34.weights_ref, bf16[2,512,1024]{2,1,0:T(8,128)(2,1)S(1)} %copy-done, ...), custom_call_target="tpu_custom_call" | custom-call | tf_op jit(solution)/shard_map/last_stage/pallas_call | solution.py:414
  (1 shorter events, 0.0 us)
Async XLA Ops:
  17.8 22.5 %collective-permute-start = (bf16[16,2,32,512]{3,2,1,0:T(8,128)(2,1)S(1)}, bf16[16,2,32,512]{3,2,1,0:T(8,128)(2,1)S(1)}, u32[]{:S(2)}, u32[]{:S(2)}) collective-permute-start(bf16[16,2,32,512]{3,2,1,0:T(8,128)(2,1)S(1)} %get-tuple-element.41.first_ref), channel_id=1, source_target_pairs={{0,1},{2,3},{4,5},{6,7},{8,9},{10,11},{12,13},{14,15},{16,17},{18,... | collective-permute-start | bytes 3145736 | tf_op jit(solution)/shard_map/ppermute | solution.py:475
  40.3 1.0 %copy-start.2 = (bf16[16,2,32,512]{3,2,1,0:T(8,128)(2,1)}, bf16[16,2,32,512]{3,2,1,0:T(8,128)(2,1)S(1)}, u32[]{:S(2)}) copy-start(bf16[16,2,32,512]{3,2,1,0:T(8,128)(2,1)S(1)} %get-tuple-element.42.second_ref) | copy-start | bytes 3145732
  41.3 24.2 %copy-start.1 = (bf16[2,1024,512]{2,1,0:T(8,128)(2,1)S(1)}, bf16[2,1024,512]{2,1,0:T(8,128)(2,1)}, u32[]{:S(2)}) copy-start(bf16[2,1024,512]{2,1,0:T(8,128)(2,1)} %down_ref.5) | copy-start | bytes 6291460
  41.3 24.2 %copy-start.3 = (bf16[2,512,512]{2,1,0:T(8,128)(2,1)S(1)}, bf16[2,512,512]{2,1,0:T(8,128)(2,1)}, u32[]{:S(2)}) copy-start(bf16[2,512,512]{2,1,0:T(8,128)(2,1)} %next_ref.1) | copy-start | bytes 3145732
  41.3 24.2 %copy-start.4 = (bf16[2,512,512]{2,1,0:T(8,128)(2,1)S(1)}, bf16[2,512,512]{2,1,0:T(8,128)(2,1)}, u32[]{:S(2)}) copy-start(bf16[2,512,512]{2,1,0:T(8,128)(2,1)} %get-tuple-element.37.dense_ref) | copy-start | bytes 3145732
  46.1 19.4 %copy-start = (bf16[2,512,1024]{2,1,0:T(8,128)(2,1)S(1)}, bf16[2,512,1024]{2,1,0:T(8,128)(2,1)}, u32[]{:S(2)}) copy-start(bf16[2,512,1024]{2,1,0:T(8,128)(2,1)} %up_ref.5) | copy-start | bytes 6291460
  66.9 21.1 %collective-permute-start.1 = (bf16[16,2,32,512]{3,2,1,0:T(8,128)(2,1)}, bf16[16,2,32,512]{3,2,1,0:T(8,128)(2,1)}, u32[]{:S(2)}, u32[]{:S(2)}) collective-permute-start(bf16[16,2,32,512]{3,2,1,0:T(8,128)(2,1)} %get-tuple-element.43.first_ref), channel_id=1, source_target_pairs={{0,1},{2,3},{4,5},{6,7},{8,9},{10,11},{12,13},{14,15},{16,17},{18,... | collective-permute-start | bytes 3145736 | tf_op jit(solution)/shard_map/ppermute | solution.py:475

commit v7 on v6

--- a/solution.py
+++ b/solution.py
@@ -258,6 +258,8 @@
     total = None
     for part in range(REACH):
         source = tile + part - before
+        if source < 0 and halo_ref is None:
+            continue
         ref, source = (arrived_ref, source) if source >= 0 else (halo_ref, source + before)
         rows = ref[tile_index(ref, source, group)].reshape(TILE, ref.shape[3])
         term = dot(band_ref[tile, part], rows)
@@ -319,9 +321,20 @@
         loads[0].wait()
 
     owners, frames, own, width = arrived_ref.shape
-    for group in range(own // GROUP):
-        for tile in range(band_ref.shape[0]):
-            put(tile, group, mix(tile, group, arrived_ref, halo_ref, band_ref), mixed_ref)
+
+    def mix_all(earlier_ref):
+        for group in range(own // GROUP):
+            for tile in range(band_ref.shape[0]):
+                mixed = mix(tile, group, arrived_ref, earlier_ref, band_ref)
+                put(tile, group, mixed, mixed_ref)
+
+    @pl.when(second_core)
+    def mix_second():
+        mix_all(halo_ref)
+
+    @pl.when(jnp.logical_not(second_core))
+    def mix_first():
+        mix_all(None)
 
     @pl.when(second_core)
     def work():

time: 93.9 us -> 93.7 us (level)
  no operation moved by 1% of the time
where the time goes in v7:
time: 93.7 us; the launch traced here: 93.3 us
  blocking collectives  74.3 us (79%)
  Pallas kernels  15 us (16%)
  starting transfers between devices  2.58 us (3%)
  local copies, waits for them, and re-layouts  1.26 us (1%)
    all_to_all x2, blocking collectives, direct(): lax.all_to_all(blocks, 'snap', split_axis=0, concat_axis=0, tiled=True)  38.8 us
    all_to_all x1, blocking collectives, across_runs(): lax.all_to_all(parted, 'snap', split_axis=0, concat_axis=0, tiled=True, a...  21.2 us
    all_to_all x1, blocking collectives, inside_runs(): lax.all_to_all(parted, 'snap', split_axis=1, concat_axis=1, tiled=True, a...  14.3 us
    pallas_call x1, Pallas kernels, last_stage(): pl.pallas_call(functools.partial(last_kernel, layer), name='last_stage',...  5.61 us
    pallas_call x1, Pallas kernels, middle_stage(): pl.pallas_call(functools.partial(middle_kernel, layer), name='middle_stag...  4.8 us
    pallas_call x1, Pallas kernels, first_graph(): pl.pallas_call(first_kernel, name='first_graph', out_shape=[in_vmem((owne...  3.23 us
    ppermute x2, starting transfers between devices, exchange_in_turn(): halo = lax.ppermute(first[-late:], 'span', [(0, 1)])  2.58 us
  transfers between devices with their start and end apart: 2, of which 0 were waited for; matrix products, arithmetic and copies ran while one was open for 0% of the time, Pallas kernels for 0%

profile of v7, /device:TPU:1, one launch (start us, length us, event | category | flops | bytes accessed | tf_op | source)
XLA Modules:
  0.0 93.3 jit_solution(3091472988555241993)
XLA Ops:
  0.0 3.2 %first_graph.1 = (bf16[16,2,32,512]{3,2,1,0:T(8,128)(2,1)S(1)}, bf16[2,512,512]{2,1,0:T(8,128)(2,1)}, f32[32,768]{1,0:T(8,128)S(1)}) custom-call(bf16[1,2,512,512]{3,2,1,0:T(8,128)(2,1)} %features_ref.1, bf16[2,512,512]{2,1,0:T(8,128)(2,1)} %next_ref.1, bf16[1,2,4,4,128,128]{5,4,3,2,1,0:T(8,128)(2,1)} %values_ref.1, s32[1,2,4,4]{3,2,1,0:T(4,128)} %cols_ref.1, ...), custom_call_target="tpu_custom_call" | custom-call | tf_op jit(solution)/shard_map/first_graph/pallas_call | solution.py:194
  3.2 14.5 %conditional.4 = (bf16[16,2,32,512]{3,2,1,0:T(8,128)(2,1)S(1)}) conditional(s32[]{:T(128)} %convert_element_type.2, bf16[16,2,32,512]{3,2,1,0:T(8,128)(2,1)S(1)} %get-tuple-element.36, bf16[16,2,32,512]{3,2,1,0:T(8,128)(2,1)S(1)} %get-tuple-element.36), branch_computations={%region_0.0_spmd, %region_1.0_spmd} | conditional | bytes 6291464 | solution.py:487
  3.2 0.1 copy.9
  3.4 14.3 %all_to_all.25 = bf16[4,4,2,32,512]{4,3,2,0,1:T(8,128)(2,1)S(1)} all-to-all(bf16[4,4,2,32,512]{4,3,2,0,1:T(8,128)(2,1)S(1)} %copy.9), channel_id=1, replica_groups={{0,2,4,6},{8,10,12,14},{16,18,20,22},{24,26,28,30},{1,3,5,7},{9,11,13,1..., dimensions={1} | all-to-all | bytes 2097152 | tf_op jit(solution)/shard_map/cond/branch_0_fun/all_to_all | solution.py:459
  17.6 0.1 copy.10
  17.8 1.3 %collective-permute-start = (bf16[16,2,32,512]{3,2,1,0:T(8,128)(2,1)S(1)}, bf16[16,2,32,512]{3,2,1,0:T(8,128)(2,1)S(1)}, u32[]{:S(2)}, u32[]{:S(2)}) collective-permute-start(bf16[16,2,32,512]{3,2,1,0:T(8,128)(2,1)S(1)} %get-tuple-element.41.first_ref), channel_id=1, source_target_pairs={{0,1},{2,3},{4,5},{6,7},{8,9},{10,11},{12,13},{14,15},{16,17},{18,... | collective-permute-start | bytes 3145736 | tf_op jit(solution)/shard_map/ppermute | solution.py:488
  19.1 21.2 %conditional.5 = (bf16[16,2,32,512]{3,2,1,0:T(8,128)(2,1)S(1)}) conditional(s32[]{:T(128)} %convert_element_type.2, bf16[16,2,32,512]{3,2,1,0:T(8,128)(2,1)S(1)} %get-tuple-element.41.first_ref, bf16[16,2,32,512]{3,2,1,0:T(8,128)(2,1)S(1)} %get-tuple-element.36), branch_computations={%region_2.0_spmd, %region_3.0_spmd} | conditional | bytes 2097160 | solution.py:490
  19.1 21.2 %all_to_all.27 = bf16[4,4,2,32,512]{4,3,2,1,0:T(8,128)(2,1)S(1)} all-to-all(bf16[4,4,2,32,512]{4,3,2,1,0:T(8,128)(2,1)S(1)} %bitcast.8), channel_id=1, replica_groups={{0,8,16,24},{2,10,18,26},{4,12,20,28},{6,14,22,30},{1,9,17,25},{3,11,19..., dimensions={0} | all-to-all | bytes 2097152 | tf_op jit(solution)/shard_map/cond/branch_0_fun/all_to_all | solution.py:473
  40.3 0.0 copy-start.2
  40.3 0.0 collective-permute-done.halo_ref
  40.3 1.0 %copy-done.2 = bf16[16,2,32,512]{3,2,1,0:T(8,128)(2,1)} copy-done((bf16[16,2,32,512]{3,2,1,0:T(8,128)(2,1)}, bf16[16,2,32,512]{3,2,1,0:T(8,128)(2,1)S(1)}, u32[]{:S(2)}) %copy-start.2) | copy-done | bytes 1048600
  41.3 0.0 copy-start.1
  41.3 0.0 copy-start.3
  41.3 0.0 copy-start.4
  41.3 4.8 %middle_stage.1 = bf16[16,2,32,512]{3,2,1,0:T(8,128)(2,1)S(1)} custom-call(bf16[16,2,32,512]{3,2,1,0:T(8,128)(2,1)S(1)} %get-tuple-element.41.first_ref, bf16[16,2,32,512]{3,2,1,0:T(8,128)(2,1)S(1)} %collective-permute-done.halo_ref, f32[32,768]{1,0:T(8,128)S(1)} %get-tuple-element.34.weights_ref, bf16[16,2,32,512]{3,2,1,0:T(8,128)(2,1)} %copy-done.2, ...), custom_call_target="tpu_custom_call" | custom-call | tf_op jit(solution)/shard_map/middle_stage/pallas_call | solution.py:355
  46.1 0.0 copy-start
  46.1 19.4 %all_to_all.30.arrived_ref = bf16[16,2,32,512]{3,2,1,0:T(8,128)(2,1)S(1)} all-to-all(bf16[16,2,32,512]{3,2,1,0:T(8,128)(2,1)S(1)} %middle_stage.1), channel_id=1, replica_groups=mesh['snap'=16,'span'=2] {'snap'}, dimensions={0} | all-to-all | bytes 2097152 | tf_op jit(solution)/shard_map/all_to_all | solution.py:446
  65.5 0.0 copy-done.1
  65.5 0.0 copy-done.3
  65.5 0.0 copy-done.4
  65.5 0.0 copy-done
  65.5 1.3 %later_graph.1 = (bf16[16,2,32,512]{3,2,1,0:T(8,128)(2,1)S(1)}, bf16[16,2,32,512]{3,2,1,0:T(8,128)(2,1)}) custom-call(bf16[16,2,32,512]{3,2,1,0:T(8,128)(2,1)S(1)} %all_to_all.30.arrived_ref, bf16[2,512,1024]{2,1,0:T(8,128)(2,1)S(1)} %copy-done, bf16[2,1024,512]{2,1,0:T(8,128)(2,1)S(1)} %copy-done.1, bf16[2,512,512]{2,1,0:T(8,128)(2,1)S(1)} %copy-done.3, ...), custom_call_target="tpu_custom_call" | custom-call | tf_op jit(solution)/shard_map/later_graph/pallas_call | solution.py:220
  66.9 1.3 %collective-permute-start.1 = (bf16[16,2,32,512]{3,2,1,0:T(8,128)(2,1)}, bf16[16,2,32,512]{3,2,1,0:T(8,128)(2,1)}, u32[]{:S(2)}, u32[]{:S(2)}) collective-permute-start(bf16[16,2,32,512]{3,2,1,0:T(8,128)(2,1)} %get-tuple-element.43.first_ref), channel_id=1, source_target_pairs={{0,1},{2,3},{4,5},{6,7},{8,9},{10,11},{12,13},{14,15},{16,17},{18,... | collective-permute-start | bytes 3145736 | tf_op jit(solution)/shard_map/ppermute | solution.py:488
  68.2 19.5 %conditional.7 = (bf16[16,2,32,512]{3,2,1,0:T(8,128)(2,1)S(1)}) conditional(s32[]{:T(128)} %convert_element_type.2, bf16[16,2,32,512]{3,2,1,0:T(8,128)(2,1)S(1)} %get-tuple-element.40, bf16[16,2,32,512]{3,2,1,0:T(8,128)(2,1)S(1)} %get-tuple-element.40), branch_computations={%region_6.0_spmd, %region_7.0_spmd} | conditional | bytes 4194312 | solution.py:490
  68.2 0.1 copy.19
  68.2 19.4 %all_to_all.29 = bf16[16,2,32,512]{3,2,1,0:T(8,128)(2,1)S(1)} all-to-all(bf16[16,2,32,512]{3,2,1,0:T(8,128)(2,1)S(1)} %copy.19), channel_id=1, replica_groups=mesh['snap'=16,'span'=2] {'snap'}, dimensions={0} | all-to-all | bytes 2097152 | tf_op jit(solution)/shard_map/cond/branch_0_fun/all_to_all | solution.py:446
  87.7 0.0 collective-permute-done.1.halo_ref
  87.7 5.6 %last_stage.1 = bf16[16,2,32,512]{3,2,1,0:T(8,128)(2,1)} custom-call(bf16[16,2,32,512]{3,2,1,0:T(8,128)(2,1)S(1)} %get-tuple-element.44.second_ref, bf16[16,2,32,512]{3,2,1,0:T(8,128)(2,1)} %collective-permute-done.1.halo_ref, f32[32,768]{1,0:T(8,128)S(1)} %get-tuple-element.34.weights_ref, bf16[2,512,1024]{2,1,0:T(8,128)(2,1)S(1)} %copy-done, ...), custom_call_target="tpu_custom_call" | custom-call | tf_op jit(solution)/shard_map/last_stage/pallas_call | solution.py:427
  (1 shorter events, 0.0 us)
Async XLA Ops:
  17.8 22.5 %collective-permute-start = (bf16[16,2,32,512]{3,2,1,0:T(8,128)(2,1)S(1)}, bf16[16,2,32,512]{3,2,1,0:T(8,128)(2,1)S(1)}, u32[]{:S(2)}, u32[]{:S(2)}) collective-permute-start(bf16[16,2,32,512]{3,2,1,0:T(8,128)(2,1)S(1)} %get-tuple-element.41.first_ref), channel_id=1, source_target_pairs={{0,1},{2,3},{4,5},{6,7},{8,9},{10,11},{12,13},{14,15},{16,17},{18,... | collective-permute-start | bytes 3145736 | tf_op jit(solution)/shard_map/ppermute | solution.py:488
  40.3 1.0 %copy-start.2 = (bf16[16,2,32,512]{3,2,1,0:T(8,128)(2,1)}, bf16[16,2,32,512]{3,2,1,0:T(8,128)(2,1)S(1)}, u32[]{:S(2)}) copy-start(bf16[16,2,32,512]{3,2,1,0:T(8,128)(2,1)S(1)} %get-tuple-element.42.second_ref) | copy-start | bytes 3145732
  41.3 24.2 %copy-start.1 = (bf16[2,1024,512]{2,1,0:T(8,128)(2,1)S(1)}, bf16[2,1024,512]{2,1,0:T(8,128)(2,1)}, u32[]{:S(2)}) copy-start(bf16[2,1024,512]{2,1,0:T(8,128)(2,1)} %down_ref.5) | copy-start | bytes 6291460
  41.3 24.2 %copy-start.3 = (bf16[2,512,512]{2,1,0:T(8,128)(2,1)S(1)}, bf16[2,512,512]{2,1,0:T(8,128)(2,1)}, u32[]{:S(2)}) copy-start(bf16[2,512,512]{2,1,0:T(8,128)(2,1)} %next_ref.1) | copy-start | bytes 3145732
  41.3 24.2 %copy-start.4 = (bf16[2,512,512]{2,1,0:T(8,128)(2,1)S(1)}, bf16[2,512,512]{2,1,0:T(8,128)(2,1)}, u32[]{:S(2)}) copy-start(bf16[2,512,512]{2,1,0:T(8,128)(2,1)} %get-tuple-element.37.dense_ref) | copy-start | bytes 3145732
  46.1 19.4 %copy-start = (bf16[2,512,1024]{2,1,0:T(8,128)(2,1)S(1)}, bf16[2,512,1024]{2,1,0:T(8,128)(2,1)}, u32[]{:S(2)}) copy-start(bf16[2,512,1024]{2,1,0:T(8,128)(2,1)} %up_ref.5) | copy-start | bytes 6291460
  66.9 20.8 %collective-permute-start.1 = (bf16[16,2,32,512]{3,2,1,0:T(8,128)(2,1)}, bf16[16,2,32,512]{3,2,1,0:T(8,128)(2,1)}, u32[]{:S(2)}, u32[]{:S(2)}) collective-permute-start(bf16[16,2,32,512]{3,2,1,0:T(8,128)(2,1)} %get-tuple-element.43.first_ref), channel_id=1, source_target_pairs={{0,1},{2,3},{4,5},{6,7},{8,9},{10,11},{12,13},{14,15},{16,17},{18,... | collective-permute-start | bytes 3145736 | tf_op jit(solution)/shard_map/ppermute | solution.py:488
